TPU v7x, 32 devices: a whole 2x2x4 slice. The times are simulated.
32 devices in a mesh: groups: 2 (over y), track: 4 (over z), frame: 2 (over x), chan: 2 (over core).
Axes of the slice: x: 2, y: 2, z: 4, core: 2. Of those that a mesh axis runs over, the one named last changes fastest.
Arguments:
- tokens: bfloat16 [512, 16, 384], P(('groups', 'track'), 'frame', 'chan'), parts along dimension 0, may hold values from -6 to 6
- track_query: bfloat16 [512, 128], P(('groups', 'track')), parts along dimension 0, may hold values from -6 to 6
- feature_map: bfloat16 [32, 1024, 128], P(('groups', 'frame'), 'track'), parts along dimension 0, may hold values from -6 to 6
- tile_ids: int32 [4, 256, 8, 1], P(('groups', 'frame'), 'track'), parts along dimension 0, may hold values from 0 to 3; in each aligned block of 256 rows (0 to 255, 256 to 511, ..., all dimensions but the last counted through in order) at most 128 rows name the same one
- corners: int32 [4, 256, 8], P(('groups', 'frame'), 'track'), parts along dimension 0, may hold values from 0 to 99
- mlp_in: bfloat16 [49, 384], replicated, may hold values from -0.875 to 0.875
- mlp_out: bfloat16 [384, 384], P(None, 'chan'), may hold values from -0.3125 to 0.3125
- cotangent: bfloat16 [512, 16, 384], P(('groups', 'track'), 'frame', 'chan'), parts along dimension 0, may hold values from -6 to 6
Outputs:
- updated: bfloat16 [512, 16, 384], P(('groups', 'track'), 'frame', 'chan'), parts along dimension 0
- tile_grad: float32 [32, 1024, 128], P(('groups', 'frame'), 'track', 'chan'), parts along dimension 0
There are 2 independent parts, one for each index of `groups`. A program takes and returns all parts, laid end to end along the dimension named above; an argument that names none is the same for every part. Nothing has to cross between parts.
Inputs may be any that keep to these rules, and one draw needn't show every extreme that they name: `tile_ids`: taking the first three dimensions in order, every aligned block of 256 rows names any one tile at most 128 times, a bound that some block reaches.
All inputs are finite; a program needn't handle non-finite values.
Results may differ from a plain program's by a relative error of at most 0.014.
Values may be sent and summed in bfloat16 or wider, within the bound.
A program may use at most 64 MiB of HBM per device.

v0:
```python
import math

import jax
import jax.numpy as jnp
from jax import lax
from jax.sharding import PartitionSpec as P

TW = 16
RAD = 3


def gelu_tanh(values):
    return jax.nn.gelu(values, approximate=True)


def scatter_rows(grad_in, query_in, base_in, map_rows, corr_scale):
    win_side = 2 * RAD + 1
    win_steps = jnp.arange(win_side, dtype=jnp.int32)
    query_wide = query_in.astype(jnp.float32)
    grad_map = jnp.zeros((map_rows, query_in.shape[2]), jnp.float32)
    for win_row in range(win_side):
        pix_index = base_in[..., None] + win_row * TW + win_steps
        picked = grad_in[:, :, win_row * win_side : (win_row + 1) * win_side].astype(jnp.float32)
        contribution = picked[..., None] * query_wide[:, :, None, :] * corr_scale
        grad_map = grad_map.at[pix_index].add(contribution)
    return grad_map


def on_device(tokens, track_query, feature_map, tile_ids, corners, mlp_in, mlp_out, cotangent):
    local_tracks, local_frames, local_width = tokens.shape
    track_count = lax.axis_size("track")
    chan_count = lax.axis_size("chan")
    chan_index = lax.axis_index("chan")
    row_count = local_tracks * local_frames
    half_rows = row_count // chan_count
    own_tracks = local_tracks // chan_count
    slot_cap = 2 * half_rows // track_count
    pixels = feature_map.shape[1]
    channels = feature_map.shape[2]
    win_side = 2 * RAD + 1
    corner_span = TW - 2 * RAD
    win_size = win_side * win_side
    corr_scale = 1.0 / math.sqrt(channels)
    tiles_flat = feature_map.reshape(local_frames * pixels, channels)
    my_query = lax.dynamic_slice_in_dim(track_query, chan_index * own_tracks, own_tracks, 0)
    tile_rows = lax.dynamic_slice_in_dim(
        tile_ids.reshape(local_tracks, local_frames), chan_index * own_tracks, own_tracks, 0
    ).reshape(half_rows)
    corner_rows = lax.dynamic_slice_in_dim(
        corners.reshape(local_tracks, local_frames), chan_index * own_tracks, own_tracks, 0
    ).reshape(half_rows)
    frame_local = jnp.tile(jnp.arange(local_frames, dtype=jnp.int32), own_tracks)
    base_pixel = frame_local * pixels + corner_rows // corner_span * TW + corner_rows % corner_span
    query_rows = jnp.repeat(my_query, local_frames, axis=0)
    dest_hits = (tile_rows[:, None] == jnp.arange(track_count, dtype=jnp.int32)[None, :]).astype(
        jnp.int32
    )
    before = jnp.cumsum(dest_hits, axis=0) - dest_hits
    target = tile_rows * slot_cap + jnp.sum(before * dest_hits, axis=1)
    query_send = (
        jnp.zeros((track_count * slot_cap, channels), jnp.bfloat16)
        .at[target]
        .set(query_rows)
        .reshape(track_count, slot_cap, channels)
    )
    base_send = (
        jnp.zeros((track_count * slot_cap,), jnp.int32)
        .at[target]
        .set(base_pixel)
        .reshape(track_count, slot_cap)
    )
    win_steps = jnp.arange(win_side, dtype=jnp.int32)
    query_in = lax.all_to_all(query_send, "track", split_axis=0, concat_axis=0, tiled=True)
    base_in = lax.all_to_all(base_send, "track", split_axis=0, concat_axis=0, tiled=True)
    pieces = []
    for win_row in range(win_side):
        pix_index = base_in[..., None] + win_row * TW + win_steps
        pieces.append(
            jnp.einsum(
                "nmsc,nmc->nms", tiles_flat[pix_index], query_in, preferred_element_type=jnp.float32
            )
        )
    corr_vals = (jnp.concatenate(pieces, axis=2) * corr_scale).astype(jnp.bfloat16)
    corr_back = lax.all_to_all(corr_vals, "track", split_axis=0, concat_axis=0, tiled=True)
    corr_back, query_in, base_in = (corr_back, query_in, base_in)
    corr_half = corr_back.reshape(track_count * slot_cap, win_size)[target]
    corr_all = lax.all_gather(corr_half, "chan", axis=0, tiled=True)
    pre_act = jnp.dot(corr_all, mlp_in, preferred_element_type=jnp.float32)
    hidden = gelu_tanh(pre_act).astype(jnp.bfloat16)
    token_rows = tokens.reshape(row_count, local_width).astype(jnp.float32)
    updated = (token_rows + jnp.dot(hidden, mlp_out, preferred_element_type=jnp.float32)).astype(
        jnp.bfloat16
    )
    updated = updated.reshape(local_tracks, local_frames, local_width)
    grad_rows = cotangent.reshape(row_count, local_width)
    summed = lax.psum(
        jnp.dot(grad_rows, mlp_out.T, preferred_element_type=jnp.float32).astype(jnp.bfloat16),
        "chan",
    ).astype(jnp.float32)
    hid_grad = lax.dynamic_slice_in_dim(summed, chan_index * half_rows, half_rows, 0)
    pre_half = lax.dynamic_slice_in_dim(pre_act, chan_index * half_rows, half_rows, 0)
    gelu_out, gelu_pull = jax.vjp(gelu_tanh, pre_half)
    pre_grad = gelu_pull(hid_grad)[0].astype(jnp.bfloat16)
    corr_grad = jnp.dot(pre_grad, mlp_in.T, preferred_element_type=jnp.float32).astype(jnp.bfloat16)
    grad_send = (
        jnp.zeros((track_count * slot_cap, win_size), jnp.bfloat16)
        .at[target]
        .set(corr_grad)
        .reshape(track_count, slot_cap, win_size)
    )
    grad_in = lax.all_to_all(grad_send, "track", split_axis=0, concat_axis=0, tiled=True)
    grad_map = scatter_rows(grad_in, query_in, base_in, local_frames * pixels, corr_scale)
    tile_grad = lax.psum_scatter(
        grad_map.reshape(local_frames, pixels, channels).astype(jnp.bfloat16),
        "chan",
        scatter_dimension=2,
        tiled=True,
    ).astype(jnp.float32)
    return (updated, tile_grad)


def solution(mesh):
    return jax.shard_map(
        on_device,
        mesh=mesh,
        in_specs=(
            P(("groups", "track"), "frame", "chan"),
            P(("groups", "track"), None),
            P(("groups", "frame"), "track", None),
            P(("groups", "frame"), "track", None, None),
            P(("groups", "frame"), "track", None),
            P(),
            P(None, "chan"),
            P(("groups", "track"), "frame", "chan"),
        ),
        out_specs=(
            P(("groups", "track"), "frame", "chan"),
            P(("groups", "frame"), "track", "chan"),
        ),
        check_vma=False,
    )
```

profile of v0, /device:TPU:0, one launch (start us, length us, event | category | flops | bytes accessed | tf_op | source)
XLA Modules:
  0.0 310.2 jit_solution(5155469118335510591)
XLA Ops:
  14.2 6.3 %all-to-all-start = ((s32[4,1,128]{2,1,0:T(1,128)}), s32[4,1,128]{2,1,0:T(1,128)S(1)}, u32[]{:S(2)}, u32[]{:S(2)}) async-start(s32[4,1,128]{2,1,0:T(1,128)} %bitcast.6), calls=%async_computation | async-start | bytes 4096 | tf_op jit(solution)/shard_map/all_to_all | solution.py:74
  26.0 4.2 %all-to-all-start.1 = ((bf16[4,128,128]{2,1,0:T(8,128)(2,1)}), bf16[4,128,128]{2,1,0:T(8,128)(2,1)S(1)}, u32[]{:S(2)}, u32[]{:S(2)}) async-start(bf16[4,128,128]{2,1,0:T(8,128)(2,1)} %bitcast.9), calls=%async_computation.1 | async-start | bytes 262144 | tf_op jit(solution)/shard_map/all_to_all | solution.py:73
  32.7 6.9 %gather_fusion.2 = bf16[3584,128]{1,0:T(8,128)(2,1)S(1)} fusion(bf16[2048,128]{1,0:T(8,128)(2,1)S(1)} %bitcast.110, s32[4096]{0:T(1024)S(1)} %get-tuple-element.36), kind=kCustom, calls=%fused_computation.2 | custom fusion | bytes 1849344 | tf_op jit(solution)/shard_map/gather | solution.py:80
  39.9 6.9 %gather_fusion.4 = bf16[3584,128]{1,0:T(8,128)(2,1)S(1)} fusion(bf16[2048,128]{1,0:T(8,128)(2,1)S(1)} %bitcast.112, s32[4096]{0:T(1024)S(1)} %get-tuple-element.34), kind=kCustom, calls=%fused_computation.4 | custom fusion | bytes 1849344 | tf_op jit(solution)/shard_map/gather | solution.py:80
  48.1 6.9 %gather_fusion.6 = bf16[3584,128]{1,0:T(8,128)(2,1)S(1)} fusion(bf16[2048,128]{1,0:T(8,128)(2,1)S(1)} %bitcast.114, s32[4096]{0:T(1024)S(1)} %get-tuple-element.32), kind=kCustom, calls=%fused_computation.6 | custom fusion | bytes 1849344 | tf_op jit(solution)/shard_map/gather | solution.py:80
  56.4 6.9 %gather_fusion = bf16[3584,128]{1,0:T(8,128)(2,1)S(1)} fusion(bf16[2048,128]{1,0:T(8,128)(2,1)S(1)} %bitcast.108, s32[4096]{0:T(1024)S(1)} %pad_clamp_fusion.6), kind=kCustom, calls=%fused_computation | custom fusion | bytes 1849344 | tf_op jit(solution)/shard_map/gather | solution.py:80
  64.6 6.9 %gather_fusion.1 = bf16[3584,128]{1,0:T(8,128)(2,1)S(1)} fusion(bf16[2048,128]{1,0:T(8,128)(2,1)S(1)} %bitcast.109, s32[4096]{0:T(1024)S(1)} %get-tuple-element.37), kind=kCustom, calls=%fused_computation.1 | custom fusion | bytes 1849344 | tf_op jit(solution)/shard_map/gather | solution.py:80
  72.8 6.9 %gather_fusion.3 = bf16[3584,128]{1,0:T(8,128)(2,1)S(1)} fusion(bf16[2048,128]{1,0:T(8,128)(2,1)S(1)} %bitcast.111, s32[4096]{0:T(1024)S(1)} %get-tuple-element.35), kind=kCustom, calls=%fused_computation.3 | custom fusion | bytes 1849344 | tf_op jit(solution)/shard_map/gather | solution.py:80
  81.0 7.1 %gather_fusion.5 = bf16[3584,128]{1,0:T(8,128)(2,1)S(1)} fusion(bf16[2048,128]{1,0:T(8,128)(2,1)S(1)} %bitcast.113, s32[4096]{0:T(1024)S(1)} %get-tuple-element.33), kind=kCustom, calls=%fused_computation.5 | custom fusion | bytes 1849344 | tf_op jit(solution)/shard_map/gather | solution.py:80
  98.7 5.1 %all-to-all-start.2 = ((bf16[4,128,49]{1,2,0:T(8,128)(2,1)}), bf16[4,128,49]{1,2,0:T(8,128)(2,1)S(1)}, u32[]{:S(2)}, u32[]{:S(2)}) async-start(bf16[4,128,49]{1,2,0:T(8,128)(2,1)} %fusion.28), calls=%async_computation.2 | async-start | bytes 114688 | tf_op jit(solution)/shard_map/all_to_all | solution.py:84
  103.8 5.7 %all-to-all-done.2 = bf16[4,128,49]{1,2,0:T(8,128)(2,1)S(1)} async-done(((bf16[4,128,49]{1,2,0:T(8,128)(2,1)}), bf16[4,128,49]{1,2,0:T(8,128)(2,1)S(1)}, u32[]{:S(2)}, u32[]{:S(2)}) %all-to-all-start.2) | async-done | bytes 50208 | tf_op jit(solution)/shard_map/all_to_all | solution.py:84
  116.4 3.3 %all-to-all-start.3 = ((bf16[4,128,49]{1,2,0:T(8,128)(2,1)}), bf16[4,128,49]{1,2,0:T(8,128)(2,1)S(1)}, u32[]{:S(2)}, u32[]{:S(2)}) async-start(bf16[4,128,49]{1,2,0:T(8,128)(2,1)} %copy.39), calls=%async_computation.3 | async-start | bytes 114688 | tf_op jit(solution)/shard_map/all_to_all | solution.py:111
  119.8 5.6 %all-to-all-done.3 = bf16[4,128,49]{1,2,0:T(8,128)(2,1)S(1)} async-done(((bf16[4,128,49]{1,2,0:T(8,128)(2,1)}), bf16[4,128,49]{1,2,0:T(8,128)(2,1)S(1)}, u32[]{:S(2)}, u32[]{:S(2)}) %all-to-all-start.3) | async-done | bytes 50208 | tf_op jit(solution)/shard_map/all_to_all | solution.py:111
  126.5 7.4 %multiply_multiply_fusion = (f32[4,128,7,128]{3,2,1,0:T(8,128)}, f32[4,128,7,128]{3,2,1,0:T(8,128)}, f32[4,128,7,128]{3,2,1,0:T(8,128)}, f32[4,128,7,128]{3,2,1,...) fusion(f32[4,128,7]{2,1,0:T(8,128)S(1)} %copy.46, ...), kind=kLoop, calls=%fused_computation.18 | loop fusion | flops 6422528 | bytes 13207552 | tf_op jit(solution)/shard_map/mul | solution.py:24
  135.6 2.6 reshape.357
  140.8 2.7 reshape.373
  151.3 20.2 %scatter_custom_fusion.3 = f32[2048,128]{1,0:T(8,128)S(1)} fusion(s32[3584]{0:T(1024)S(1)} %reshape.259, f32[3584,128]{1,0:T(8,128)} %reshape.349, f32[]{:T(128)} %constant.21.clone.1), kind=kCustom, calls=%fused_computation.47 | custom fusion | flops 458752 | bytes 1049088 | tf_op jit(solution)/shard_map/scatter-add | solution.py:25
  171.6 20.6 %scatter_fusion = f32[2048,128]{1,0:T(8,128)S(1)} fusion(f32[2048,128]{1,0:T(8,128)S(1)} %scatter_custom_fusion.3, s32[3584]{0:T(1024)S(1)} %reshape.267, f32[3584,128]{1,0:T(8,128)} %reshape.357), kind=kCustom, calls=%fused_computation.12 | custom fusion | flops 458752 | bytes 5519360 | tf_op jit(solution)/shard_map/scatter-add | solution.py:25
  192.1 20.4 %scatter_fusion.1 = f32[2048,128]{1,0:T(8,128)S(1)} fusion(f32[2048,128]{1,0:T(8,128)S(1)} %scatter_fusion, s32[3584]{0:T(1024)S(1)} %reshape.275, f32[3584,128]{1,0:T(8,128)} %reshape.365), kind=kCustom, calls=%fused_computation.13 | custom fusion | flops 458752 | bytes 5519360 | tf_op jit(solution)/shard_map/scatter-add | solution.py:25
  212.5 20.4 %scatter_fusion.2 = f32[2048,128]{1,0:T(8,128)S(1)} fusion(f32[2048,128]{1,0:T(8,128)S(1)} %scatter_fusion.1, s32[3584]{0:T(1024)S(1)} %reshape.283, f32[3584,128]{1,0:T(8,128)} %reshape.373), kind=kCustom, calls=%fused_computation.14 | custom fusion | flops 458752 | bytes 5519360 | tf_op jit(solution)/shard_map/scatter-add | solution.py:25
  232.9 20.4 %scatter_fusion.3 = f32[2048,128]{1,0:T(8,128)S(1)} fusion(f32[2048,128]{1,0:T(8,128)S(1)} %scatter_fusion.2, s32[3584]{0:T(1024)S(1)} %reshape.291, f32[3584,128]{1,0:T(8,128)} %reshape.381), kind=kCustom, calls=%fused_computation.15 | custom fusion | flops 458752 | bytes 5519360 | tf_op jit(solution)/shard_map/scatter-add | solution.py:25
  253.2 20.4 %scatter_fusion.4 = f32[2048,128]{1,0:T(8,128)S(1)} fusion(f32[2048,128]{1,0:T(8,128)S(1)} %scatter_fusion.3, s32[3584]{0:T(1024)S(1)} %reshape.299, f32[3584,128]{1,0:T(8,128)} %reshape.389), kind=kCustom, calls=%fused_computation.16 | custom fusion | flops 458752 | bytes 5519360 | tf_op jit(solution)/shard_map/scatter-add | solution.py:25
  273.6 20.0 %scatter_fusion.5 = f32[2048,128]{1,0:T(8,128)S(1)} fusion(f32[2048,128]{1,0:T(8,128)S(1)} %scatter_fusion.4, s32[3584]{0:T(1024)S(1)} %reshape.307, f32[3584,128]{1,0:T(8,128)S(1)} %reshape.397), kind=kCustom, calls=%fused_computation.17 | custom fusion | flops 458752 | bytes 5519360 | tf_op jit(solution)/shard_map/scatter-add | solution.py:25
  296.5 5.0 %reduce-scatter.2.cloned.1.call-done = bf16[8,256,64]{1,0,2:T(8,128)(2,1)} async-done(((bf16[8,256,128]{1,0,2:T(8,128)(2,1)}), bf16[8,256,64]{1,0,2:T(8,128)(2,1)}) %reduce-scatter.2.cloned.1.call-update) | async-done | bytes 262160 | tf_op jit(solution)/shard_map/reduce_scatter | solution.py:113
  (136 shorter events, 56.6 us)
Async XLA Ops:
  7.2 25.5 %copy-start = (bf16[8,256,128]{2,1,0:T(8,128)(2,1)S(1)}, bf16[8,256,128]{2,1,0:T(8,128)(2,1)}, u32[]{:S(2)}) copy-start(bf16[8,256,128]{2,1,0:T(8,128)(2,1)} %param.10) | copy-start | bytes 1572868
  14.2 11.7 %all-to-all-start = ((s32[4,1,128]{2,1,0:T(1,128)}), s32[4,1,128]{2,1,0:T(1,128)S(1)}, u32[]{:S(2)}, u32[]{:S(2)}) async-start(s32[4,1,128]{2,1,0:T(1,128)} %bitcast.6), calls=%async_computation | async-start | bytes 4096 | tf_op jit(solution)/shard_map/all_to_all | solution.py:74
  20.6 92.1 %all-reduce.2.cloned.1.call-start = ((), (), s32[]{:S(2)}) async-start(), calls=%async_computation.5 | async-start | bytes 786432 | tf_op jit(solution)/shard_map/psum | solution.py:96
  26.0 63.5 %all-to-all-start.1 = ((bf16[4,128,128]{2,1,0:T(8,128)(2,1)}), bf16[4,128,128]{2,1,0:T(8,128)(2,1)S(1)}, u32[]{:S(2)}, u32[]{:S(2)}) async-start(bf16[4,128,128]{2,1,0:T(8,128)(2,1)} %bitcast.9), calls=%async_computation.1 | async-start | bytes 262144 | tf_op jit(solution)/shard_map/all_to_all | solution.py:73
  90.1 2.2 copy-start.1
  92.3 3.0 copy-start.2
  93.1 3.0 copy-start.3
  96.0 1.2 copy-start.4
  96.8 15.6 %copy-start.9 = (bf16[49,384]{1,0:T(8,128)(2,1)S(1)}, bf16[49,384]{1,0:T(8,128)(2,1)}, u32[]{:S(2)}) copy-start(bf16[49,384]{1,0:T(8,128)(2,1)} %param.13) | copy-start | bytes 112900
  98.7 10.8 %all-to-all-start.2 = ((bf16[4,128,49]{1,2,0:T(8,128)(2,1)}), bf16[4,128,49]{1,2,0:T(8,128)(2,1)S(1)}, u32[]{:S(2)}, u32[]{:S(2)}) async-start(bf16[4,128,49]{1,2,0:T(8,128)(2,1)} %fusion.28), calls=%async_computation.2 | async-start | bytes 114688 | tf_op jit(solution)/shard_map/all_to_all | solution.py:84
  112.7 7.0 %copy-start.5 = (f32[512,384]{1,0:T(8,128)}, f32[512,384]{1,0:T(8,128)S(1)}, u32[]{:S(2)}) copy-start(f32[512,384]{1,0:T(8,128)S(1)} %fusion.68) | copy-start | bytes 2359300
  116.4 9.0 %all-to-all-start.3 = ((bf16[4,128,49]{1,2,0:T(8,128)(2,1)}), bf16[4,128,49]{1,2,0:T(8,128)(2,1)S(1)}, u32[]{:S(2)}, u32[]{:S(2)}) async-start(bf16[4,128,49]{1,2,0:T(8,128)(2,1)} %copy.39), calls=%async_computation.3 | async-start | bytes 114688 | tf_op jit(solution)/shard_map/all_to_all | solution.py:111
  119.7 181.9 %reduce-scatter.2.cloned.1.call-start = ((), (), s32[]{:S(2)}) async-start(), calls=%async_computation.6 | async-start | bytes 786432 | tf_op jit(solution)/shard_map/reduce_scatter | solution.py:113
  293.6 1.3 copy-start.7
  293.7 1.5 copy-start.6
  293.7 1.5 copy-start.8
Sparse Core Ops, SparseCore 0:
  24.3 19.9 all-reduce.1
  295.1 6.4 reduce-scatter.1
where the time goes:
time: 311 us; the launch traced here: 310 us
  other arithmetic  155 us (50%)
  local copies, waits for them, and re-layouts  90.6 us (29%)
  starting transfers between devices  19 us (6%)
  waiting for transfers between devices  17.3 us (6%)
  between operations  14.6 us (5%)
  matrix products  11.7 us (4%)
    scatter-add x7, other arithmetic, scatter_rows(): grad_map = grad_map.at[pix_index].add(contribution)  142 us
    gather x14, local copies, waits for them, and re-layouts, on_device(): tiles_flat[pix_index]  56.7 us
    mul x7, local copies, waits for them, and re-layouts, scatter_rows(): contribution = picked[..., None] * query_wide[:, :, None, :] * corr_scale  17.4 us
    mul x1, other arithmetic, scatter_rows(): contribution = picked[..., None] * query_wide[:, :, None, :] * corr_scale  7.44 us
    dot_general x7, matrix products, on_device(): jnp.einsum('nmsc,nmc->nms', tiles_flat[pix_index], query_in, preferred_el...  7.41 us
    all_to_all x1, starting transfers between devices, on_device(): lax.all_to_all(base_send, 'track', split_axis=0, concat_axis=0, tiled=True)  6.32 us
  transfers between devices with their start and end apart: 6, of which 4 were waited for; matrix products, arithmetic and copies ran while one was open for 24% of the time, Pallas kernels for 0%

commit v1 on v0

v1 whole, which is shorter than its diff:
```python
import functools
import math

import jax
import jax.numpy as jnp
from jax import lax
from jax.experimental import pallas as pl
from jax.experimental.pallas import tpu as pltpu
from jax.sharding import PartitionSpec as P

TW = 16
RAD = 3
SIDE = 2 * RAD + 1
SPAN = TW - 2 * RAD
BF = jnp.bfloat16
F32 = jnp.float32
I32 = jnp.int32
MESH = pl.DeviceIdType.MESH


def each(count, body):
    if count <= 8:
        for step in range(count):
            body(step)
    else:
        def step_body(step, carry):
            body(step)
            return carry

        lax.fori_loop(0, count, step_body, 0)


def iota(shape, dim):
    return lax.broadcasted_iota(I32, shape, dim)


def onehot(cond):
    return jnp.where(cond, 1.0, 0.0).astype(BF)


def mm(a, b, ca=1, cb=0):
    return lax.dot_general(a, b, (((ca,), (cb,)), ((), ())), preferred_element_type=F32)


def pick(values, index):
    return jnp.take_along_axis(values, index, axis=1, mode="promise_in_bounds")


def gelu_parts(x):
    k0 = math.sqrt(2.0 / math.pi)
    k1 = 0.044715
    sq = x * x
    th = jnp.tanh(k0 * (x + k1 * (sq * x)))
    return sq, th


def kernel(n_track, tok_ref, qry_ref, fmap_ref, tile_ref, corner_ref, win_ref, wout_ref, cot_ref,
           upd_ref, tg_ref,
           qb_ref, loc_ref, wi_ref, sendw_ref, recvw_ref, xs_ref, gh_ref, ghs_ref, gho_ref, gs_ref, recvg_ref,
           qp_ref, tgs_ref,
           q_ssem, q_rsem, w_ssem, w_rsem, g_ssem, g_rsem, x_ssem, x_rsem, h_ssem, h_rsem, t_ssem, t_rsem):
    z = lax.axis_index("track")
    c = lax.axis_index("chan")
    me = z * 2 + c
    peers = 2 * n_track
    sib = {"chan": 1 - c}
    scale = 1.0 / math.sqrt(qry_ref.shape[1])
    group = min(n_track, 4)
    chunk_rows = group * 64
    n_chunks = n_track // group

    barrier = pltpu.get_barrier_semaphore()

    def greet(step):
        peer = lax.rem(me + step + 1, peers)
        pl.semaphore_signal(barrier, inc=1, device_id={"track": peer // 2, "chan": lax.rem(peer, 2)},
                            device_id_type=MESH)

    each(peers - 1, greet)

    corner = corner_ref[...]
    crow = (corner * 205) >> 11
    base = (crow * (TW - SPAN) + corner).astype(F32).astype(BF)
    tile = tile_ref[...].astype(F32).astype(BF)
    e1 = onehot(iota((8, 128), 0) == iota((8, 128), 1))
    e2 = onehot(iota((8, 128), 0) + 8 == iota((8, 128), 1))
    qb_ref[z, :, 0:128] = qry_ref[...]
    qb_ref[z, :, 128:256] = (mm(base, e1) + mm(tile, e2)).astype(BF)

    pl.semaphore_wait(barrier, peers - 1)

    def q_copy(step, slot):
        return pltpu.make_async_remote_copy(
            src_ref=qb_ref.at[slot], dst_ref=qb_ref.at[slot], send_sem=q_ssem.at[step], recv_sem=q_rsem.at[step],
            device_id={"track": lax.rem(z + step + 1, n_track)}, device_id_type=MESH)

    each(n_track - 1, lambda step: q_copy(step, z).start())

    wout = wout_ref[...]
    rows = 256
    oth = pl.multiple_of((1 - c) * rows, rows)
    own = pl.multiple_of(c * rows, rows)
    ghs_ref[...] = mm(cot_ref[pl.ds(oth, rows), :], wout, 1, 1).astype(BF)
    h_copy = pltpu.make_async_remote_copy(src_ref=ghs_ref, dst_ref=gh_ref, send_sem=h_ssem, recv_sem=h_rsem,
                                          device_id=sib, device_id_type=MESH)
    h_copy.start()
    gho_ref[...] = mm(cot_ref[pl.ds(own, rows), :], wout, 1, 1).astype(BF)

    wst = mm(onehot((iota((128, 49), 0) & 63) == iota((128, 49), 1)), win_ref[...]).astype(BF)

    each(n_track - 1, lambda step: q_copy(step, lax.rem(z + n_track - 1 - step, n_track)).wait_recv())

    lane = iota((chunk_rows, 128), 1)
    low = lane < 64
    wlane = lane & 63
    wrow = (wlane * 37) >> 8
    off = jnp.where(wlane < SIDE * SIDE, wrow * (TW - SIDE) + wlane, 0)
    krow = iota((128, 128), 0)

    def forward(k):
        k0 = k * group
        r0 = k * chunk_rows if isinstance(k, int) else pl.multiple_of(k * chunk_rows, chunk_rows)
        qry = qb_ref[pl.ds(k0, group), :, 0:128].reshape(chunk_rows, 128)
        tbl = qb_ref[pl.ds(k0, group), :, 128:256].reshape(chunk_rows, 128)
        for j in range(2):
            vals, locs = [], []
            for f in (j, j + 2):
                t = c * 4 + f
                sel = jnp.where(krow == t, 1.0, jnp.where(krow == t + 8, 256.0, 0.0)).astype(BF)
                loc = mm(tbl, sel).astype(I32) - z * 256
                loc_ref[f, pl.ds(r0, chunk_rows), :] = loc
                locs.append(loc)
                vals.append(mm(qry, fmap_ref[t], 1, 1) * scale)
            loc = jnp.where(low, locs[0], locs[1])
            idx = loc + off
            ix = idx & 127
            hi = (idx & 128) != 0
            got = [jnp.where(hi, pick(v[:, 128:256], ix), pick(v[:, 0:128], ix)) for v in vals]
            val = jnp.where(low, got[0], got[1])
            val = jnp.where((loc >= 0) & (loc < 256), val, 0.0).astype(BF)
            sendw_ref[pl.ds(k0, group), :, j * 32:(j + 1) * 32, :] = val.reshape(group, 2, 32, 128)

    each(n_chunks, forward)

    def w_copy(step, slot):
        peer = lax.rem(me + step + 1, peers)
        return pltpu.make_async_remote_copy(
            src_ref=sendw_ref.at[peer // 2, lax.rem(peer, 2)], dst_ref=recvw_ref.at[slot],
            send_sem=w_ssem.at[step], recv_sem=w_rsem.at[step],
            device_id={"track": peer // 2, "chan": lax.rem(peer, 2)}, device_id_type=MESH)

    each(peers - 1, lambda step: w_copy(step, me).start())
    recvw_ref[me] = sendw_ref[z, c]

    def maps(k):
        k0 = k * group
        r0 = k * chunk_rows if isinstance(k, int) else pl.multiple_of(k * chunk_rows, chunk_rows)
        qry = qb_ref[pl.ds(k0, group), :, 0:128].reshape(chunk_rows, 128)
        turn = onehot(((iota((128, 128), 0) + c * 64) & 127) == iota((128, 128), 1))
        qp_ref[pl.ds(r0, chunk_rows), :] = mm(qry, turn).astype(BF)
        for f in range(4):
            loc = loc_ref[f, pl.ds(r0, chunk_rows), :]
            for half in range(2):
                p = lane + half * 128
                dr = (p >> 4) - (loc >> 4)
                dc = (p & 15) - (loc & 15)
                ok = (dr >= 0) & (dr < SIDE) & (dc >= 0) & (dc < SIDE)
                wi_ref[f, half, pl.ds(r0, chunk_rows), :] = jnp.where(ok, dr * SIDE + dc + 64 * (f // 2), -1)

    each(n_chunks, maps)

    each(peers - 1, lambda step: w_copy(step, lax.rem(me + peers - 1 - step, peers)).wait_recv())

    def gathered(part):
        if n_track <= 8:
            total = recvw_ref[part].astype(F32)
            for src in range(1, n_track):
                total = total + recvw_ref[src * 2 + part].astype(F32)
            return total
        return lax.fori_loop(0, n_track, lambda src, acc: acc + recvw_ref[src * 2 + part].astype(F32),
                             jnp.zeros((64, 128), F32))

    for part in range(2):
        xs_ref[0, part * 64:(part + 1) * 64, :] = gathered(part).astype(BF)
    x_copy = pltpu.make_async_remote_copy(src_ref=xs_ref.at[0], dst_ref=xs_ref.at[1], send_sem=x_ssem,
                                          recv_sem=x_rsem, device_id=sib, device_id_type=MESH)
    x_copy.start()

    tok_row, tok_col = iota((256, 128), 0), iota((256, 128), 1)
    t_of = tok_row & 7
    spread = onehot(tok_col == ((t_of >> 2) << 6) + ((t_of & 1) << 5) + (tok_row >> 3))
    keep = ((t_of >> 1) & 1) == (tok_col >> 6)
    q_row, q_col = iota((128, 256), 0), iota((128, 256), 1)
    u_of = q_col & 7
    fold = onehot(q_row == ((u_of >> 2) << 6) + ((u_of & 1) << 5) + (q_col >> 3))

    def first_layer(slot):
        return mm(jnp.where(keep, mm(spread, xs_ref[slot]), 0.0).astype(BF), wst)

    def finish(pre, th, start):
        hidden = (0.5 * pre * (1.0 + th)).astype(BF)
        upd_ref[pl.ds(start, rows), :] = (tok_ref[pl.ds(start, rows), :].astype(F32) + mm(hidden, wout)).astype(BF)

    pre = first_layer(0)
    sq, th = gelu_parts(pre)
    slope = 0.5 * (1.0 + th) + (0.5 * math.sqrt(2.0 / math.pi)) * pre * (1.0 - th * th) * (1.0 + 3 * 0.044715 * sq)
    h_copy.wait_recv()
    hid = gho_ref[...].astype(F32) + gh_ref[...].astype(F32)
    pre_grad = (hid * slope).astype(BF)
    cg = jnp.where(keep, mm(pre_grad, wst, 1, 1), 0.0).astype(BF)
    gs_ref[...] = mm(fold, cg).astype(BF).reshape(2, 64, 128)

    def g_copy(step, slot):
        peer = lax.rem(me + step + 1, peers)
        return pltpu.make_async_remote_copy(
            src_ref=gs_ref.at[lax.rem(peer, 2)], dst_ref=recvg_ref.at[slot],
            send_sem=g_ssem.at[step], recv_sem=g_rsem.at[step],
            device_id={"track": peer // 2, "chan": lax.rem(peer, 2)}, device_id_type=MESH)

    each(peers - 1, lambda step: g_copy(step, me).start())
    recvg_ref[me] = gs_ref[c]

    finish(pre, th, own)
    x_copy.wait_recv()
    pre = first_layer(1)
    sq, th = gelu_parts(pre)
    finish(pre, th, oth)

    each(peers - 1, lambda step: g_copy(step, lax.rem(me + peers - 1 - step, peers)).wait_recv())

    t_copies = []
    for f in range(4):
        j = f % 2

        def cells(k, f=f, j=j):
            k0 = k * group * 2
            r0 = k * chunk_rows if isinstance(k, int) else pl.multiple_of(k * chunk_rows, chunk_rows)
            g = recvg_ref[pl.ds(k0, group * 2), j * 32:(j + 1) * 32, :].reshape(chunk_rows, 128).astype(F32)
            qp = qp_ref[pl.ds(r0, chunk_rows), :]
            halves = []
            for half in range(2):
                wi = wi_ref[f, half, pl.ds(r0, chunk_rows), :]
                placed = jnp.where(wi >= 0, pick(g, wi & 127), 0.0).astype(BF)
                halves.append(mm(placed, qp, 0, 0))
            return jnp.concatenate(halves, axis=0)

        if n_chunks == 1:
            total = cells(0)
        else:
            total = lax.fori_loop(0, n_chunks, lambda k, acc: acc + cells(k), jnp.zeros((256, 128), F32))
        total = total * scale
        t = c * 4 + f
        tg_ref[t] = total[:, 0:64]
        tgs_ref[f] = total[:, 64:128]
        copy = pltpu.make_async_remote_copy(src_ref=tgs_ref.at[f], dst_ref=tg_ref.at[t], send_sem=t_ssem.at[f],
                                            recv_sem=t_rsem.at[f], device_id=sib, device_id_type=MESH)
        copy.start()
        t_copies.append(copy)

    each(n_track - 1, lambda step: q_copy(step, z).wait_send())
    h_copy.wait_send()
    each(peers - 1, lambda step: w_copy(step, me).wait_send())
    x_copy.wait_send()
    each(peers - 1, lambda step: g_copy(step, me).wait_send())
    for f in range(4):
        t_copies[f].wait_send()
        pltpu.make_async_remote_copy(src_ref=tgs_ref.at[f], dst_ref=tg_ref.at[(1 - c) * 4 + f], send_sem=t_ssem.at[f],
                                     recv_sem=t_rsem.at[f], device_id=sib, device_id_type=MESH).wait_recv()


def on_device(tokens, track_query, feature_map, tile_ids, corners, mlp_in, mlp_out, cotangent):
    local_tracks, local_frames, width = tokens.shape
    n_track = lax.axis_size("track")
    rows = local_tracks * local_frames
    pixels, channels = feature_map.shape[1:]
    hid = mlp_in.shape[1]
    peers = 2 * n_track
    all_tracks = n_track * local_tracks
    dma = pltpu.SemaphoreType.DMA
    vmem = pltpu.VMEM
    upd, tg = pl.pallas_call(
        functools.partial(kernel, n_track),
        out_shape=(
            jax.ShapeDtypeStruct((rows, width), BF),
            jax.ShapeDtypeStruct((local_frames, pixels, channels // 2), F32),
        ),
        in_specs=[pl.BlockSpec(memory_space=vmem)] * 8,
        out_specs=(pl.BlockSpec(memory_space=vmem), pl.BlockSpec(memory_space=vmem)),
        scratch_shapes=[
            vmem((n_track, local_tracks, 256), BF),
            vmem((4, all_tracks, 128), I32),
            vmem((4, 2, all_tracks, 128), I32),
            vmem((n_track, 2, 64, 128), BF),
            vmem((peers, 64, 128), BF),
            vmem((2, 128, 128), BF),
            vmem((256, hid), BF),
            vmem((256, hid), BF),
            vmem((256, hid), BF),
            vmem((2, 64, 128), BF),
            vmem((peers, 64, 128), BF),
            vmem((all_tracks, 128), BF),
            vmem((4, pixels, channels // 2), F32),
            dma((n_track - 1,)), dma((n_track - 1,)),
            dma((peers - 1,)), dma((peers - 1,)),
            dma((peers - 1,)), dma((peers - 1,)),
            dma, dma, dma, dma,
            dma((4,)), dma((4,)),
        ],
        compiler_params=pltpu.CompilerParams(collective_id=0, has_side_effects=True,
                                             vmem_limit_bytes=48 * 1024 * 1024),
        cost_estimate=pl.CostEstimate(flops=10**9, bytes_accessed=4 * 10**6, transcendentals=2 * 10**5),
        name="corr_step",
    )(
        tokens.reshape(rows, width), track_query, feature_map, tile_ids.reshape(local_tracks, local_frames),
        corners.reshape(local_tracks, local_frames), mlp_in, mlp_out, cotangent.reshape(rows, width),
    )
    return upd.reshape(tokens.shape), tg


def solution(mesh):
    return jax.shard_map(
        on_device,
        mesh=mesh,
        in_specs=(
            P(("groups", "track"), "frame", "chan"),
            P(("groups", "track"), None),
            P(("groups", "frame"), "track", None),
            P(("groups", "frame"), "track", None, None),
            P(("groups", "frame"), "track", None),
            P(),
            P(None, "chan"),
            P(("groups", "track"), "frame", "chan"),
        ),
        out_specs=(
            P(("groups", "track"), "frame", "chan"),
            P(("groups", "frame"), "track", "chan"),
        ),
        check_vma=False,
    )
```

time: 311 us -> 30.6 us (0.10)
  other arithmetic: 155 us -> 0 us
  local copies, waits for them, and re-layouts: 90.6 us -> 6.46 us
  Pallas kernels: 0 us -> 23.1 us
  starting transfers between devices: 19 us -> 0 us
  waiting for transfers between devices: 17.3 us -> 0 us
  between operations: 14.6 us -> 0.69 us
  matrix products: 11.7 us -> 0 us
    scatter-add x7 -> x0, other arithmetic: 142 us -> none  [scatter_rows(): grad_map = grad_map.at[pix_index].add(contribution)]
    gather x15 -> x0, local copies, waits for them, and re-layouts: 57.5 us -> none  [the longest x14 56.7 us: on_device(): tiles_flat[pix_index]]
    pallas_call x0 -> x1, Pallas kernels: none -> 23.1 us  [on_device(): pl.pallas_call(functools.partial(kernel, n_track), out_shape=(jax.ShapeDt...]
    all_to_all x4 -> x0, starting transfers between devices: 18.9 us -> none  [the longest x1 6.32 us: on_device(): lax.all_to_all(base_send, 'track', split_axis=0, concat_axis=0, tiled=True)]
    mul x10 -> x0, local copies, waits for them, and re-layouts: 17.6 us -> none  [the longest x7 17.4 us: scatter_rows(): contribution = picked[..., None] * query_wide[:, :, None, :] * corr_scale]
    all_to_all x4 -> x0, waiting for transfers between devices: 12.2 us -> none  [the longest x1 5.71 us: on_device(): lax.all_to_all(corr_vals, 'track', split_axis=0, concat_axis=0, tiled=True)]
    dot_general x11 -> x0, matrix products: 11.7 us -> none  [the longest x7 7.41 us: on_device(): jnp.einsum('nmsc,nmc->nms', tiles_flat[pix_index], query_in, preferred_el...]
    mul x3 -> x0, other arithmetic: 8.2 us -> none  [the longest x1 7.44 us: scatter_rows(): contribution = picked[..., None] * query_wide[:, :, None, :] * corr_scale]
  transfers between devices with their start and end apart: 6 -> 0, of which waited for: 4 -> 0; matrix products, arithmetic and copies ran while one was open for 24% -> 0% of each run, Pallas kernels for 0% -> 0%
where the time goes in v1:
time: 30.6 us; the launch traced here: 30.3 us
  Pallas kernels  23.1 us (75%)
  local copies, waits for them, and re-layouts  6.46 us (21%)
  between operations  0.69 us (2%)
    pallas_call x1, Pallas kernels, on_device(): pl.pallas_call(functools.partial(kernel, n_track), out_shape=(jax.ShapeDt...  23.1 us
    unnamed x15, local copies, waits for them, and re-layouts  6.46 us

profile of v1, /device:TPU:0, one launch (start us, length us, event | category | flops | bytes accessed | tf_op | source)
XLA Modules:
  0.0 30.3 jit_solution(4399326876051394171)
XLA Ops:
  0.6 0.0 copy-start.1
  0.6 0.8 %copy.10 = s32[1,64,8,1]{2,1,3,0:T(8,128)S(1)} copy(s32[1,64,8,1]{1,3,2,0:T(1,128)} %param.11) | data formatting | bytes 4096 | tf_op args[3]
  1.5 0.8 %copy.11 = s32[1,64,8]{2,1,0:T(8,128)S(1)} copy(s32[1,64,8]{1,2,0:T(8,128)} %param.12) | data formatting | bytes 4096 | tf_op args[4]
  2.2 0.0 copy-start.3
  2.2 0.0 copy-start.4
  2.2 1.1 %copy.12.wout_ref = bf16[384,192]{1,0:T(8,128)(2,1)S(1)} copy(bf16[384,192]{0,1:T(8,128)(2,1)} %param.14) | data formatting | bytes 294912 | tf_op args[6]
  3.3 0.0 copy-done.1
  3.3 0.0 copy-done.3
  3.3 0.0 copy-done.4
  3.3 0.0 copy-start
  3.3 1.0 %copy-done = bf16[8,256,128]{2,1,0:T(8,128)(2,1)S(1)} copy-done((bf16[8,256,128]{2,1,0:T(8,128)(2,1)S(1)}, bf16[8,256,128]{2,1,0:T(8,128)(2,1)}, u32[]{:S(2)}) %copy-start) | copy-done | bytes 524312
  4.4 0.0 copy-start.2
  4.4 0.9 %copy-done.2 = bf16[64,8,192]{2,1,0:T(8,128)(2,1)S(1)} copy-done((bf16[64,8,192]{2,1,0:T(8,128)(2,1)S(1)}, bf16[64,8,192]{2,1,0:T(8,128)(2,1)}, u32[]{:S(2)}) %copy-start.2) | copy-done | bytes 196632
  5.3 23.1 %corr_step.1 = (bf16[512,192]{1,0:T(8,128)(2,1)S(1)}, f32[8,256,64]{2,1,0:T(8,128)S(1)}) custom-call(bf16[512,192]{1,0:T(8,128)(2,1)S(1)} %bitcast.8, bf16[64,128]{1,0:T(8,128)(2,1)S(1)} %copy-done.4, bf16[8,256,128]{2,1,0:T(8,128)(2,1)S(1)} %copy-done, s32[64,8]{1,0:T(8,128)S(1)} %bitcast.6, s32[64,8]{1,0:T(8,128)S(1)} %bitcast.7, ...), custom_call_target="tpu_custom_call" | custom-call | flops 1000000000 | bytes 4000000 | tf_op jit(solution)/shard_map/corr_step/pallas_call | solution.py:281
  28.5 1.1 %copy.13 = f32[8,256,64]{1,2,0:T(8,128)} copy(f32[8,256,64]{2,1,0:T(8,128)S(1)} %get-tuple-element.7) | data formatting | bytes 1048576
  29.6 0.7 %copy.15 = bf16[64,8,192]{2,1,0:T(8,128)(2,1)} copy(bf16[64,8,192]{2,1,0:T(8,128)(2,1)S(1)} %bitcast.5) | data formatting | bytes 393216
Async XLA Ops:
  0.6 2.7 %copy-start.1 = (bf16[64,8,192]{2,1,0:T(8,128)(2,1)S(1)}, bf16[64,8,192]{2,1,0:T(8,128)(2,1)}, u32[]{:S(2)}) copy-start(bf16[64,8,192]{2,1,0:T(8,128)(2,1)} %param.8) | copy-start | bytes 589828
  2.2 1.1 %copy-start.3 = (bf16[49,384]{1,0:T(8,128)(2,1)S(1)}, bf16[49,384]{1,0:T(8,128)(2,1)}, u32[]{:S(2)}) copy-start(bf16[49,384]{1,0:T(8,128)(2,1)} %win_ref.1) | copy-start | bytes 112900
  2.2 1.1 %copy-start.4 = (bf16[64,128]{1,0:T(8,128)(2,1)S(1)}, bf16[64,128]{1,0:T(8,128)(2,1)}, u32[]{:S(2)}) copy-start(bf16[64,128]{1,0:T(8,128)(2,1)} %qry_ref.1) | copy-start | bytes 49156
  3.3 1.0 %copy-start = (bf16[8,256,128]{2,1,0:T(8,128)(2,1)S(1)}, bf16[8,256,128]{2,1,0:T(8,128)(2,1)}, u32[]{:S(2)}) copy-start(bf16[8,256,128]{2,1,0:T(8,128)(2,1)} %fmap_ref.1) | copy-start | bytes 1572868
  4.4 0.9 %copy-start.2 = (bf16[64,8,192]{2,1,0:T(8,128)(2,1)S(1)}, bf16[64,8,192]{2,1,0:T(8,128)(2,1)}, u32[]{:S(2)}) copy-start(bf16[64,8,192]{2,1,0:T(8,128)(2,1)} %param.15) | copy-start | bytes 589828

commit v2 on v1

v2 whole, which is shorter than its diff:
```python
import functools
import math

import jax
import jax.numpy as jnp
from jax import lax
from jax.experimental import pallas as pl
from jax.experimental.pallas import tpu as pltpu
from jax.sharding import PartitionSpec as P

TW = 16
RAD = 3
SIDE = 2 * RAD + 1
SPAN = TW - 2 * RAD
BF = jnp.bfloat16
F32 = jnp.float32
I32 = jnp.int32
MESH = pl.DeviceIdType.MESH


def each(count, body):
    if count <= 8:
        for step in range(count):
            body(step)
    else:
        def step_body(step, carry):
            body(step)
            return carry

        lax.fori_loop(0, count, step_body, 0)


def iota(shape, dim):
    return lax.broadcasted_iota(I32, shape, dim)


def onehot(cond):
    return jnp.where(cond, 1.0, 0.0).astype(BF)


def mm(a, b, ca=1, cb=0):
    return lax.dot_general(a, b, (((ca,), (cb,)), ((), ())), preferred_element_type=F32)


def pick(values, index):
    return jnp.take_along_axis(values, index, axis=1, mode="promise_in_bounds")


def gelu_parts(x):
    k0 = math.sqrt(2.0 / math.pi)
    k1 = 0.044715
    sq = x * x
    th = jnp.tanh(k0 * (x + k1 * (sq * x)))
    return sq, th


def kernel(n_track, tok_hbm, qry_hbm, fmap_hbm, tile_hbm, corner_hbm, win_hbm, wout_hbm, cot_hbm,
           upd_ref, tg_ref,
           tok_ref, qry_ref, fmap_ref, tile_ref, corner_ref, win_ref, wout_ref, cot_ref,
           qb_ref, corr_ref, loc_ref, wi_ref, sendw_ref, recvw_ref, xs_ref, gh_ref, ghs_ref, gho_ref, gs_ref,
           recvg_ref, gm_ref, qt_ref, tgs_ref,
           in_sem, q_ssem, q_rsem, w_ssem, w_rsem, g_ssem, g_rsem, x_ssem, x_rsem, h_ssem, h_rsem, t_ssem, t_rsem):
    loads = [pltpu.make_async_copy(src, dst, in_sem.at[i]) for i, (src, dst) in enumerate((
        (tile_hbm, tile_ref), (corner_hbm, corner_ref), (qry_hbm, qry_ref), (cot_hbm, cot_ref), (wout_hbm, wout_ref),
        (fmap_hbm, fmap_ref), (win_hbm, win_ref), (tok_hbm, tok_ref)))]
    for load in loads:
        load.start()
    z = lax.axis_index("track")
    c = lax.axis_index("chan")
    me = z * 2 + c
    peers = 2 * n_track
    sib = {"chan": 1 - c}
    scale = 1.0 / math.sqrt(qry_ref.shape[1])
    group = min(n_track, 4)
    chunk_rows = group * 64
    n_chunks = n_track // group

    barrier = pltpu.get_barrier_semaphore()

    def greet(step):
        peer = lax.rem(me + step + 1, peers)
        pl.semaphore_signal(barrier, inc=1, device_id={"track": peer // 2, "chan": lax.rem(peer, 2)},
                            device_id_type=MESH)

    each(peers - 1, greet)

    for load in loads[:3]:
        load.wait()
    corner = corner_ref[...]
    crow = (corner * 205) >> 11
    base = (crow * (TW - SPAN) + corner).astype(F32).astype(BF)
    tile = tile_ref[:, 0, :].astype(F32).astype(BF)
    wide = onehot(iota((64, 128), 0) == iota((64, 128), 1))
    qb_ref[z, 0:64, :] = qry_ref[...]
    qb_ref[z, 64:80, :] = jnp.concatenate([mm(base, wide), mm(tile, wide)], axis=0).astype(BF)

    pl.semaphore_wait(barrier, peers - 1)

    def q_copy(step, slot):
        return pltpu.make_async_remote_copy(
            src_ref=qb_ref.at[slot], dst_ref=qb_ref.at[slot], send_sem=q_ssem.at[step], recv_sem=q_rsem.at[step],
            device_id={"track": lax.rem(z + step + 1, n_track)}, device_id_type=MESH)

    each(n_track - 1, lambda step: q_copy(step, z).start())

    for load in loads[3:]:
        load.wait()
    wout = wout_ref[...]
    rows = 256
    oth = pl.multiple_of((1 - c) * rows, rows)
    own = pl.multiple_of(c * rows, rows)
    ghs_ref[...] = mm(cot_ref[pl.ds(oth, rows), :], wout).astype(BF)
    h_copy = pltpu.make_async_remote_copy(src_ref=ghs_ref, dst_ref=gh_ref, send_sem=h_ssem, recv_sem=h_rsem,
                                          device_id=sib, device_id_type=MESH)
    h_copy.start()
    gho_ref[...] = mm(cot_ref[pl.ds(own, rows), :], wout).astype(BF)

    wst = mm(onehot((iota((128, 49), 0) & 63) == iota((128, 49), 1)), win_ref[...]).astype(BF)

    each(n_track - 1, lambda step: q_copy(step, lax.rem(z + n_track - 1 - step, n_track)).wait_recv())

    lane = iota((64, 128), 1)
    low = lane < 64
    wlane = lane & 63
    wrow = (wlane * 37) >> 8
    off = jnp.where(wlane < SIDE * SIDE, wrow * (TW - SIDE) + wlane, 0)
    krow = iota((128, 128), 0)
    eye16 = onehot(iota((16, 128), 0) == iota((16, 128), 1))

    def row_of(k, size):
        return k * size if isinstance(k, int) else pl.multiple_of(k * size, size)

    def forward(k):
        k0 = k * group
        r0 = row_of(k, chunk_rows)
        qry = qb_ref[pl.ds(k0, group), 0:64, :].reshape(chunk_rows, 128)
        tbl = jnp.concatenate([mm(qb_ref[k0 + i, 64:80, :], eye16, 0, 0)[0:64] for i in range(group)], axis=0).astype(BF)
        for f in range(4):
            t = c * 4 + f
            sel = jnp.where(krow == t, 1.0, jnp.where(krow == t + 8, 256.0, 0.0)).astype(BF)
            loc_ref[f, pl.ds(r0, chunk_rows), :] = mm(tbl, sel).astype(I32) - z * 256
            corr_ref[f, pl.ds(r0, chunk_rows), :] = mm(qry, fmap_ref[t], 1, 1) * scale

    each(n_chunks, forward)

    def w_copy(step, to, slot_z, part, sems, slot_c):
        return pltpu.make_async_remote_copy(
            src_ref=sendw_ref.at[to, part], dst_ref=recvw_ref.at[slot_z * 2 + slot_c],
            send_sem=w_ssem.at[step * 2 + part], recv_sem=w_rsem.at[step * 2 + sems],
            device_id={"track": to, "chan": part}, device_id_type=MESH)

    def windows(to):
        r0 = pl.multiple_of(to * 64, 64)
        for j in range(2):
            locs = [loc_ref[f, pl.ds(r0, 64), :] for f in (j, j + 2)]
            loc = jnp.where(low, locs[0], locs[1])
            idx = loc + off
            ix = idx & 127
            hi = (idx & 128) != 0
            got = [jnp.where(hi, pick(corr_ref[f, pl.ds(r0, 64), 128:256], ix),
                             pick(corr_ref[f, pl.ds(r0, 64), 0:128], ix)) for f in (j, j + 2)]
            val = jnp.where(low, got[0], got[1])
            val = jnp.where((loc >= 0) & (loc < 256), val, 0.0).astype(BF)
            sendw_ref[to, :, j * 32:(j + 1) * 32, :] = val.reshape(2, 32, 128)

    def w_send(step):
        to = lax.rem(z + step + 1, n_track)
        windows(to)
        for part in range(2):
            w_copy(step, to, z, part, c, c).start()

    each(n_track - 1, w_send)
    windows(z)
    last = n_track - 1

    def sib_copy(buf_src, buf_dst, ssem, rsem):
        return pltpu.make_async_remote_copy(
            src_ref=buf_src, dst_ref=buf_dst, send_sem=ssem.at[last * 2 + 1 - c], recv_sem=rsem.at[last * 2 + c],
            device_id=sib, device_id_type=MESH)

    def sib_wait(buf_src, buf_dst, ssem, rsem):
        return pltpu.make_async_remote_copy(
            src_ref=buf_src, dst_ref=buf_dst, send_sem=ssem.at[last * 2 + 1 - c], recv_sem=rsem.at[last * 2 + 1 - c],
            device_id=sib, device_id_type=MESH)

    sib_copy(sendw_ref.at[z, 1 - c], recvw_ref.at[me], w_ssem, w_rsem).start()
    recvw_ref[me] = sendw_ref[z, c]

    eye = onehot(krow == iota((128, 128), 1))
    clane = iota((chunk_rows, 128), 1)

    def maps(k):
        r0 = row_of(k, chunk_rows)
        qry = qb_ref[pl.ds(k * group, group), 0:64, :].reshape(chunk_rows, 128)
        qt_ref[:, pl.ds(r0, chunk_rows)] = mm(eye, qry, 1, 1).astype(BF)
        for f in range(4):
            loc = loc_ref[f, pl.ds(r0, chunk_rows), :]
            for half in range(2):
                p = clane + half * 128
                dr = (p >> 4) - (loc >> 4)
                dc = (p & 15) - (loc & 15)
                ok = (dr >= 0) & (dr < SIDE) & (dc >= 0) & (dc < SIDE)
                wi_ref[f, half, pl.ds(r0, chunk_rows), :] = jnp.where(ok, dr * SIDE + dc + 64 * (f // 2), -1)

    each(n_chunks, maps)

    tok_row, tok_col = iota((256, 128), 0), iota((256, 128), 1)
    t_of = tok_row & 7
    spread = onehot(tok_col == ((t_of >> 2) << 6) + ((t_of & 1) << 5) + (tok_row >> 3))
    keep = ((t_of >> 1) & 1) == (tok_col >> 6)
    q_row, q_col = iota((128, 256), 0), iota((128, 256), 1)
    u_of = q_col & 7
    fold = onehot(q_row == ((u_of >> 2) << 6) + ((u_of & 1) << 5) + (q_col >> 3))

    def w_wait(step):
        src = lax.rem(z + n_track - 1 - step, n_track)
        for part in range(2):
            w_copy(step, src, src, part, part, part).wait_recv()

    sib_wait(sendw_ref.at[z, 1 - c], recvw_ref.at[z * 2 + 1 - c], w_ssem, w_rsem).wait_recv()
    each(n_track - 1, w_wait)

    def gathered(part):
        if n_track <= 8:
            total = recvw_ref[part].astype(F32)
            for src in range(1, n_track):
                total = total + recvw_ref[src * 2 + part].astype(F32)
            return total
        return lax.fori_loop(0, n_track, lambda src, acc: acc + recvw_ref[src * 2 + part].astype(F32),
                             jnp.zeros((64, 128), F32))

    for part in range(2):
        xs_ref[0, part * 64:(part + 1) * 64, :] = gathered(part).astype(BF)
    x_copy = pltpu.make_async_remote_copy(src_ref=xs_ref.at[0], dst_ref=xs_ref.at[1], send_sem=x_ssem,
                                          recv_sem=x_rsem, device_id=sib, device_id_type=MESH)
    x_copy.start()

    def first_layer(slot):
        return mm(jnp.where(keep, mm(spread, xs_ref[slot]), 0.0).astype(BF), wst)

    def finish(pre, th, start):
        hidden = (0.5 * pre * (1.0 + th)).astype(BF)
        upd_ref[pl.ds(start, rows), :] = (
            tok_ref[pl.ds(start, rows), :].astype(F32) + mm(hidden, wout, 1, 1)).astype(BF)

    pre = first_layer(0)
    sq, th = gelu_parts(pre)
    slope = 0.5 * (1.0 + th) + (0.5 * math.sqrt(2.0 / math.pi)) * pre * (1.0 - th * th) * (1.0 + 3 * 0.044715 * sq)
    h_copy.wait_recv()
    hid = gho_ref[...].astype(F32) + gh_ref[...].astype(F32)
    pre_grad = (hid * slope).astype(BF)
    cg = jnp.where(keep, mm(pre_grad, wst, 1, 1), 0.0).astype(BF)
    gs_ref[...] = mm(fold, cg).astype(BF).reshape(2, 64, 128)

    def g_copy(step, to, slot_z, part, sems, slot_c):
        return pltpu.make_async_remote_copy(
            src_ref=gs_ref.at[part], dst_ref=recvg_ref.at[slot_z * 2 + slot_c],
            send_sem=g_ssem.at[step * 2 + part], recv_sem=g_rsem.at[step * 2 + sems],
            device_id={"track": to, "chan": part}, device_id_type=MESH)

    def g_send(step):
        for part in range(2):
            g_copy(step, lax.rem(z + step + 1, n_track), z, part, c, c).start()

    each(n_track - 1, g_send)
    sib_copy(gs_ref.at[1 - c], recvg_ref.at[me], g_ssem, g_rsem).start()
    recvg_ref[me] = gs_ref[c]

    finish(pre, th, own)
    x_copy.wait_recv()
    pre = first_layer(1)
    sq, th = gelu_parts(pre)
    finish(pre, th, oth)

    def place(src):
        r0 = pl.multiple_of(src * 64, 64)
        for f in range(4):
            j = f % 2
            g = recvg_ref[pl.ds(src * 2, 2), j * 32:(j + 1) * 32, :].reshape(64, 128).astype(F32)
            for half in range(2):
                wi = wi_ref[f, half, pl.ds(r0, 64), :]
                gm_ref[f, pl.ds(r0, 64), half * 128:(half + 1) * 128] = jnp.where(
                    wi >= 0, pick(g, wi & 127), 0.0).astype(BF)

    sib_wait(gs_ref.at[1 - c], recvg_ref.at[z * 2 + 1 - c], g_ssem, g_rsem).wait_recv()
    place(z)

    def g_take(step):
        src = lax.rem(z + n_track - 1 - step, n_track)
        for part in range(2):
            g_copy(step, src, src, part, part, part).wait_recv()
        place(src)

    each(n_track - 1, g_take)

    half_ch = tg_ref.shape[1]
    theirs = pl.multiple_of((1 - c) * half_ch, half_ch)
    mine = pl.multiple_of(c * half_ch, half_ch)

    def t_copy(f, t):
        return pltpu.make_async_remote_copy(src_ref=tgs_ref.at[f, pl.ds(theirs, half_ch), :], dst_ref=tg_ref.at[t],
                                            send_sem=t_ssem.at[f], recv_sem=t_rsem.at[f], device_id=sib,
                                            device_id_type=MESH)

    for f in range(4):
        tgs_ref[f] = mm(qt_ref[...], gm_ref[f]) * scale
        t_copy(f, c * 4 + f).start()
        tg_ref[c * 4 + f] = tgs_ref[f, pl.ds(mine, half_ch), :]

    each(n_track - 1, lambda step: q_copy(step, z).wait_send())
    h_copy.wait_send()
    x_copy.wait_send()
    sib_copy(sendw_ref.at[z, 1 - c], recvw_ref.at[me], w_ssem, w_rsem).wait_send()
    sib_copy(gs_ref.at[1 - c], recvg_ref.at[me], g_ssem, g_rsem).wait_send()

    def sent(step):
        to = lax.rem(z + step + 1, n_track)
        for part in range(2):
            w_copy(step, to, z, part, c, c).wait_send()
            g_copy(step, to, z, part, c, c).wait_send()

    each(n_track - 1, sent)
    for f in range(4):
        t_copy(f, c * 4 + f).wait_send()
        t_copy(f, (1 - c) * 4 + f).wait_recv()


def hand_out(upd_ref, tg_ref, upd_out, tg_out, sem):
    copies = [pltpu.make_async_copy(tg_ref, tg_out, sem.at[0]), pltpu.make_async_copy(upd_ref, upd_out, sem.at[1])]
    for copy in copies:
        copy.start()
    for copy in copies:
        copy.wait()


def on_device(tokens, track_query, feature_map, tile_ids, corners, mlp_in, mlp_out, cotangent):
    local_tracks, local_frames, width = tokens.shape
    n_track = lax.axis_size("track")
    rows = local_tracks * local_frames
    pixels, channels = feature_map.shape[1:]
    hid = mlp_in.shape[1]
    peers = 2 * n_track
    all_tracks = n_track * local_tracks
    dma = pltpu.SemaphoreType.DMA
    vmem = pltpu.VMEM
    args = (
        tokens.reshape(rows, width), track_query, feature_map,
        jnp.transpose(tile_ids, (0, 2, 3, 1)).reshape(local_frames, 1, local_tracks),
        jnp.transpose(corners, (0, 2, 1)).reshape(local_frames, local_tracks), mlp_in, mlp_out.T,
        cotangent.reshape(rows, width),
    )
    outs = (
        jax.ShapeDtypeStruct((rows, width), BF),
        jax.ShapeDtypeStruct((local_frames, channels // 2, pixels), F32),
    )
    upd, tg = pl.pallas_call(
        functools.partial(kernel, n_track),
        out_shape=outs,
        in_specs=[pl.BlockSpec(memory_space=pltpu.HBM)] * 8,
        out_specs=(pl.BlockSpec(memory_space=vmem), pl.BlockSpec(memory_space=vmem)),
        scratch_shapes=[vmem(arg.shape, arg.dtype) for arg in args] + [
            vmem((n_track, 80, 128), BF),
            vmem((4, all_tracks, pixels), F32),
            vmem((4, all_tracks, 128), I32),
            vmem((4, 2, all_tracks, 128), I32),
            vmem((n_track, 2, 64, 128), BF),
            vmem((peers, 64, 128), BF),
            vmem((2, 128, 128), BF),
            vmem((256, hid), BF),
            vmem((256, hid), BF),
            vmem((256, hid), BF),
            vmem((2, 64, 128), BF),
            vmem((peers, 64, 128), BF),
            vmem((4, all_tracks, pixels), BF),
            vmem((channels, all_tracks), BF),
            vmem((4, channels, pixels), F32),
            dma((8,)),
            dma((n_track - 1,)), dma((n_track - 1,)),
            dma((peers,)), dma((peers,)),
            dma((peers,)), dma((peers,)),
            dma, dma, dma, dma,
            dma((4,)), dma((4,)),
        ],
        compiler_params=pltpu.CompilerParams(collective_id=0, has_side_effects=True,
                                             vmem_limit_bytes=48 * 1024 * 1024),
        cost_estimate=pl.CostEstimate(flops=10**9, bytes_accessed=4 * 10**6, transcendentals=2 * 10**5),
        name="corr_step",
    )(*[pltpu.with_memory_space_constraint(arg, pltpu.HBM) for arg in args])
    upd, tg = pl.pallas_call(
        hand_out,
        out_shape=outs,
        in_specs=[pl.BlockSpec(memory_space=vmem)] * 2,
        out_specs=(pl.BlockSpec(memory_space=pltpu.HBM), pl.BlockSpec(memory_space=pltpu.HBM)),
        scratch_shapes=[dma((2,))],
        name="hand_out",
    )(upd, tg)
    return upd.reshape(tokens.shape), jnp.transpose(tg, (0, 2, 1))


def solution(mesh):
    return jax.shard_map(
        on_device,
        mesh=mesh,
        in_specs=(
            P(("groups", "track"), "frame", "chan"),
            P(("groups", "track"), None),
            P(("groups", "frame"), "track", None),
            P(("groups", "frame"), "track", None, None),
            P(("groups", "frame"), "track", None),
            P(),
            P(None, "chan"),
            P(("groups", "track"), "frame", "chan"),
        ),
        out_specs=(
            P(("groups", "track"), "frame", "chan"),
            P(("groups", "frame"), "track", "chan"),
        ),
        check_vma=False,
    )
```

time: 30.6 us -> 25.7 us (0.84)
  local copies, waits for them, and re-layouts: 6.46 us -> 1.47 us
    unnamed x15 -> x4, local copies, waits for them, and re-layouts: 6.46 us -> 1.47 us
    pallas_call x1 -> x2, Pallas kernels: 23.1 us -> 23.4 us  [the longest x1 21.4 us: on_device(): pl.pallas_call(functools.partial(kernel, n_track), out_shape=outs, in_spe...]
where the time goes in v2:
time: 25.7 us; the launch traced here: 25.5 us
  Pallas kernels  23.4 us (91%)
  local copies, waits for them, and re-layouts  1.47 us (6%)
  between operations  0.65 us (3%)
    pallas_call x1, Pallas kernels, on_device(): pl.pallas_call(functools.partial(kernel, n_track), out_shape=outs, in_spe...  21.4 us
    pallas_call x1, Pallas kernels, on_device(): pl.pallas_call(hand_out, out_shape=outs, in_specs=[pl.BlockSpec(memory_sp...  2.01 us
    unnamed x4, local copies, waits for them, and re-layouts  1.47 us

profile of v2, /device:TPU:0, one launch (start us, length us, event | category | flops | bytes accessed | tf_op | source)
XLA Modules:
  0.0 25.5 jit_solution(592223002906401984)
XLA Ops:
  0.6 21.4 %corr_step.1 = (bf16[512,192]{1,0:T(8,128)(2,1)S(1)}, f32[8,64,256]{2,1,0:T(8,128)S(1)}) custom-call(bf16[512,192]{1,0:T(8,128)(2,1)} %bitcast.14, bf16[64,128]{1,0:T(8,128)(2,1)} %qry_hbm.1, bf16[8,256,128]{2,1,0:T(8,128)(2,1)} %fmap_hbm.1, s32[8,1,64]{2,1,0:T(1,128)} %bitcast.18, s32[8,64]{1,0:T(8,128)} %bitcast.19, bf16[49,384]{1,0:T(8,128)(2,1)} %win_hbm.1, ...), custom_call_target="tpu_custom_call" | custom-call | flops 1000000000 | bytes 4000000 | tf_op jit(solution)/shard_map/corr_step/pallas_call | solution.py:356
  22.0 0.0 copy-start
  22.1 0.8 %copy-done = f32[8,64,256]{2,1,0:T(8,128)} copy-done((f32[8,64,256]{2,1,0:T(8,128)}, f32[8,64,256]{2,1,0:T(8,128)S(1)}, u32[]{:S(2)}) %copy-start) | copy-done | bytes 524312
  22.8 0.0 copy-start.1
  22.8 0.7 %copy-done.1 = bf16[512,192]{1,0:T(8,128)(2,1)} copy-done((bf16[512,192]{1,0:T(8,128)(2,1)}, bf16[512,192]{1,0:T(8,128)(2,1)S(1)}, u32[]{:S(2)}) %copy-start.1) | copy-done | bytes 196632
  23.5 2.0 %hand_out.1 = (bf16[512,192]{1,0:T(8,128)(2,1)}, f32[8,64,256]{2,1,0:T(8,128)}) custom-call(bf16[512,192]{1,0:T(8,128)(2,1)} %copy-done.1, f32[8,64,256]{2,1,0:T(8,128)} %copy-done), custom_call_target="tpu_custom_call" | custom-call | tf_op jit(solution)/shard_map/hand_out/pallas_call | solution.py:389
Async XLA Ops:
  22.0 0.8 %copy-start = (f32[8,64,256]{2,1,0:T(8,128)}, f32[8,64,256]{2,1,0:T(8,128)S(1)}, u32[]{:S(2)}) copy-start(f32[8,64,256]{2,1,0:T(8,128)S(1)} %get-tuple-element.7.tg_ref) | copy-start | bytes 1572868
  22.8 0.7 %copy-start.1 = (bf16[512,192]{1,0:T(8,128)(2,1)}, bf16[512,192]{1,0:T(8,128)(2,1)S(1)}, u32[]{:S(2)}) copy-start(bf16[512,192]{1,0:T(8,128)(2,1)S(1)} %get-tuple-element.6.upd_ref) | copy-start | bytes 589828

commit v3 on v2

--- a/solution.py
+++ b/solution.py
@@ -55,11 +55,11 @@
 
 
 def kernel(n_track, tok_hbm, qry_hbm, fmap_hbm, tile_hbm, corner_hbm, win_hbm, wout_hbm, cot_hbm,
-           upd_ref, tg_ref,
+           upd_hbm, tg_hbm,
            tok_ref, qry_ref, fmap_ref, tile_ref, corner_ref, win_ref, wout_ref, cot_ref,
            qb_ref, corr_ref, loc_ref, wi_ref, sendw_ref, recvw_ref, xs_ref, gh_ref, ghs_ref, gho_ref, gs_ref,
-           recvg_ref, gm_ref, qt_ref, tgs_ref,
-           in_sem, q_ssem, q_rsem, w_ssem, w_rsem, g_ssem, g_rsem, x_ssem, x_rsem, h_ssem, h_rsem, t_ssem, t_rsem):
+           recvg_ref, gm_ref, qt_ref, tgs_ref, upd_ref,
+           in_sem, out_sem, q_ssem, q_rsem, w_ssem, w_rsem, g_ssem, g_rsem, x_ssem, x_rsem, h_ssem, h_rsem, t_ssem, t_rsem):
     loads = [pltpu.make_async_copy(src, dst, in_sem.at[i]) for i, (src, dst) in enumerate((
         (tile_hbm, tile_ref), (corner_hbm, corner_ref), (qry_hbm, qry_ref), (cot_hbm, cot_ref), (wout_hbm, wout_ref),
         (fmap_hbm, fmap_ref), (win_hbm, win_ref), (tok_hbm, tok_ref)))]
@@ -143,10 +143,10 @@
 
     each(n_chunks, forward)
 
-    def w_copy(step, to, slot_z, part, sems, slot_c):
+    def w_copy(step, piece, to, slot_z, part, sems, slot_c):
         return pltpu.make_async_remote_copy(
-            src_ref=sendw_ref.at[to, part], dst_ref=recvw_ref.at[slot_z * 2 + slot_c],
-            send_sem=w_ssem.at[step * 2 + part], recv_sem=w_rsem.at[step * 2 + sems],
+            src_ref=sendw_ref.at[to, part, piece], dst_ref=recvw_ref.at[slot_z * 2 + slot_c, piece],
+            send_sem=w_ssem.at[piece, step * 2 + part], recv_sem=w_rsem.at[piece, step * 2 + sems],
             device_id={"track": to, "chan": part}, device_id_type=MESH)
 
     def windows(to):
@@ -161,29 +161,34 @@
                              pick(corr_ref[f, pl.ds(r0, 64), 0:128], ix)) for f in (j, j + 2)]
             val = jnp.where(low, got[0], got[1])
             val = jnp.where((loc >= 0) & (loc < 256), val, 0.0).astype(BF)
-            sendw_ref[to, :, j * 32:(j + 1) * 32, :] = val.reshape(2, 32, 128)
+            sendw_ref[to, :, :, j * 16:(j + 1) * 16, :] = val.reshape(2, 2, 16, 128)
 
     def w_send(step):
         to = lax.rem(z + step + 1, n_track)
         windows(to)
         for part in range(2):
-            w_copy(step, to, z, part, c, c).start()
+            w_copy(step, 0, to, z, part, c, c).start()
+
+    def w_send_rest(step):
+        for part in range(2):
+            w_copy(step, 1, lax.rem(z + step + 1, n_track), z, part, c, c).start()
+
+    last = n_track - 1
+
+    def sib_copy(buf_src, buf_dst, ssem, rsem, piece, sems):
+        return pltpu.make_async_remote_copy(
+            src_ref=buf_src, dst_ref=buf_dst, send_sem=ssem.at[piece, last * 2 + 1 - c],
+            recv_sem=rsem.at[piece, last * 2 + sems], device_id=sib, device_id_type=MESH)
+
+    def w_sib(piece, slot_c):
+        return sib_copy(sendw_ref.at[z, 1 - c, piece], recvw_ref.at[z * 2 + slot_c, piece], w_ssem, w_rsem, piece,
+                        slot_c)
 
     each(n_track - 1, w_send)
     windows(z)
-    last = n_track - 1
-
-    def sib_copy(buf_src, buf_dst, ssem, rsem):
-        return pltpu.make_async_remote_copy(
-            src_ref=buf_src, dst_ref=buf_dst, send_sem=ssem.at[last * 2 + 1 - c], recv_sem=rsem.at[last * 2 + c],
-            device_id=sib, device_id_type=MESH)
-
-    def sib_wait(buf_src, buf_dst, ssem, rsem):
-        return pltpu.make_async_remote_copy(
-            src_ref=buf_src, dst_ref=buf_dst, send_sem=ssem.at[last * 2 + 1 - c], recv_sem=rsem.at[last * 2 + 1 - c],
-            device_id=sib, device_id_type=MESH)
-
-    sib_copy(sendw_ref.at[z, 1 - c], recvw_ref.at[me], w_ssem, w_rsem).start()
+    w_sib(0, c).start()
+    each(n_track - 1, w_send_rest)
+    w_sib(1, c).start()
     recvw_ref[me] = sendw_ref[z, c]
 
     eye = onehot(krow == iota((128, 128), 1))
@@ -204,133 +209,147 @@
 
     each(n_chunks, maps)
 
-    tok_row, tok_col = iota((256, 128), 0), iota((256, 128), 1)
+    half_rows = rows // 2
+    tok_row = iota((half_rows, 64), 0)
     t_of = tok_row & 7
-    spread = onehot(tok_col == ((t_of >> 2) << 6) + ((t_of & 1) << 5) + (tok_row >> 3))
-    keep = ((t_of >> 1) & 1) == (tok_col >> 6)
-    q_row, q_col = iota((128, 256), 0), iota((128, 256), 1)
+    spread = onehot(iota((half_rows, 64), 1) == ((t_of >> 2) << 5) + ((t_of & 1) << 4) + (tok_row >> 3))
+    keep = ((iota((half_rows, 128), 0) >> 1) & 1) == (iota((half_rows, 128), 1) >> 6)
+    q_col = iota((64, half_rows), 1)
     u_of = q_col & 7
-    fold = onehot(q_row == ((u_of >> 2) << 6) + ((u_of & 1) << 5) + (q_col >> 3))
-
-    def w_wait(step):
-        src = lax.rem(z + n_track - 1 - step, n_track)
+    fold = onehot(iota((64, half_rows), 0) == ((u_of >> 2) << 5) + ((u_of & 1) << 4) + (q_col >> 3))
+
+    def gathered(piece, part):
+        if n_track <= 8:
+            total = recvw_ref[part, piece].astype(F32)
+            for src in range(1, n_track):
+                total = total + recvw_ref[src * 2 + part, piece].astype(F32)
+            return total
+        return lax.fori_loop(0, n_track, lambda src, acc: acc + recvw_ref[src * 2 + part, piece].astype(F32),
+                             jnp.zeros((32, 128), F32))
+
+    def first_layer(slot, piece):
+        return mm(jnp.where(keep, mm(spread, xs_ref[slot, piece]), 0.0).astype(BF), wst)
+
+    def finish(pre, th, start):
+        start = pl.multiple_of(start, half_rows)
+        hidden = (0.5 * pre * (1.0 + th)).astype(BF)
+        upd_ref[pl.ds(start, half_rows), :] = (
+            tok_ref[pl.ds(start, half_rows), :].astype(F32) + mm(hidden, wout, 1, 1)).astype(BF)
+
+    def g_copy(step, piece, to, slot_z, part, sems, slot_c):
+        return pltpu.make_async_remote_copy(
+            src_ref=gs_ref.at[piece, part], dst_ref=recvg_ref.at[slot_z * 2 + slot_c, piece],
+            send_sem=g_ssem.at[piece, step * 2 + part], recv_sem=g_rsem.at[piece, step * 2 + sems],
+            device_id={"track": to, "chan": part}, device_id_type=MESH)
+
+    def g_sib(piece, slot_c):
+        return sib_copy(gs_ref.at[piece, 1 - c], recvg_ref.at[z * 2 + slot_c, piece], g_ssem, g_rsem, piece, slot_c)
+
+    kept = []
+    for piece in range(2):
+        w_sib(piece, 1 - c).wait_recv()
+
+        def w_wait(step, piece=piece):
+            src = lax.rem(z + n_track - 1 - step, n_track)
+            for part in range(2):
+                w_copy(step, piece, src, src, part, part, part).wait_recv()
+
+        each(n_track - 1, w_wait)
         for part in range(2):
-            w_copy(step, src, src, part, part, part).wait_recv()
-
-    sib_wait(sendw_ref.at[z, 1 - c], recvw_ref.at[z * 2 + 1 - c], w_ssem, w_rsem).wait_recv()
-    each(n_track - 1, w_wait)
-
-    def gathered(part):
-        if n_track <= 8:
-            total = recvw_ref[part].astype(F32)
-            for src in range(1, n_track):
-                total = total + recvw_ref[src * 2 + part].astype(F32)
-            return total
-        return lax.fori_loop(0, n_track, lambda src, acc: acc + recvw_ref[src * 2 + part].astype(F32),
-                             jnp.zeros((64, 128), F32))
-
-    for part in range(2):
-        xs_ref[0, part * 64:(part + 1) * 64, :] = gathered(part).astype(BF)
+            xs_ref[0, piece, part * 32:(part + 1) * 32, :] = gathered(piece, part).astype(BF)
+        pre = first_layer(0, piece)
+        sq, th = gelu_parts(pre)
+        slope = 0.5 * (1.0 + th) + (0.5 * math.sqrt(2.0 / math.pi)) * pre * (1.0 - th * th) * (
+            1.0 + 3 * 0.044715 * sq)
+        if piece == 0:
+            h_copy.wait_recv()
+        here = slice(piece * half_rows, (piece + 1) * half_rows)
+        hid = gho_ref[here, :].astype(F32) + gh_ref[here, :].astype(F32)
+        pre_grad = (hid * slope).astype(BF)
+        cg = jnp.where(keep, mm(pre_grad, wst, 1, 1), 0.0).astype(BF)
+        gs_ref[piece] = mm(fold, cg).astype(BF).reshape(2, 32, 128)
+
+        def g_send(step, piece=piece):
+            for part in range(2):
+                g_copy(step, piece, lax.rem(z + step + 1, n_track), z, part, c, c).start()
+
+        each(n_track - 1, g_send)
+        g_sib(piece, c).start()
+        recvg_ref[me, piece] = gs_ref[piece, c]
+        kept.append((pre, th))
+
     x_copy = pltpu.make_async_remote_copy(src_ref=xs_ref.at[0], dst_ref=xs_ref.at[1], send_sem=x_ssem,
                                           recv_sem=x_rsem, device_id=sib, device_id_type=MESH)
     x_copy.start()
-
-    def first_layer(slot):
-        return mm(jnp.where(keep, mm(spread, xs_ref[slot]), 0.0).astype(BF), wst)
-
-    def finish(pre, th, start):
-        hidden = (0.5 * pre * (1.0 + th)).astype(BF)
-        upd_ref[pl.ds(start, rows), :] = (
-            tok_ref[pl.ds(start, rows), :].astype(F32) + mm(hidden, wout, 1, 1)).astype(BF)
-
-    pre = first_layer(0)
-    sq, th = gelu_parts(pre)
-    slope = 0.5 * (1.0 + th) + (0.5 * math.sqrt(2.0 / math.pi)) * pre * (1.0 - th * th) * (1.0 + 3 * 0.044715 * sq)
-    h_copy.wait_recv()
-    hid = gho_ref[...].astype(F32) + gh_ref[...].astype(F32)
-    pre_grad = (hid * slope).astype(BF)
-    cg = jnp.where(keep, mm(pre_grad, wst, 1, 1), 0.0).astype(BF)
-    gs_ref[...] = mm(fold, cg).astype(BF).reshape(2, 64, 128)
-
-    def g_copy(step, to, slot_z, part, sems, slot_c):
-        return pltpu.make_async_remote_copy(
-            src_ref=gs_ref.at[part], dst_ref=recvg_ref.at[slot_z * 2 + slot_c],
-            send_sem=g_ssem.at[step * 2 + part], recv_sem=g_rsem.at[step * 2 + sems],
-            device_id={"track": to, "chan": part}, device_id_type=MESH)
-
-    def g_send(step):
-        for part in range(2):
-            g_copy(step, lax.rem(z + step + 1, n_track), z, part, c, c).start()
-
-    each(n_track - 1, g_send)
-    sib_copy(gs_ref.at[1 - c], recvg_ref.at[me], g_ssem, g_rsem).start()
-    recvg_ref[me] = gs_ref[c]
-
-    finish(pre, th, own)
+    for piece in range(2):
+        finish(*kept[piece], own + piece * half_rows)
     x_copy.wait_recv()
-    pre = first_layer(1)
-    sq, th = gelu_parts(pre)
-    finish(pre, th, oth)
+    for piece in range(2):
+        pre = first_layer(1, piece)
+        finish(pre, gelu_parts(pre)[1], oth + piece * half_rows)
+    upd_copy = pltpu.make_async_copy(upd_ref, upd_hbm, out_sem.at[4])
+    upd_copy.start()
 
     def place(src):
         r0 = pl.multiple_of(src * 64, 64)
         for f in range(4):
             j = f % 2
-            g = recvg_ref[pl.ds(src * 2, 2), j * 32:(j + 1) * 32, :].reshape(64, 128).astype(F32)
+            g = recvg_ref[pl.ds(src * 2, 2), :, j * 16:(j + 1) * 16, :].reshape(64, 128).astype(F32)
             for half in range(2):
                 wi = wi_ref[f, half, pl.ds(r0, 64), :]
                 gm_ref[f, pl.ds(r0, 64), half * 128:(half + 1) * 128] = jnp.where(
                     wi >= 0, pick(g, wi & 127), 0.0).astype(BF)
 
-    sib_wait(gs_ref.at[1 - c], recvg_ref.at[z * 2 + 1 - c], g_ssem, g_rsem).wait_recv()
+    for piece in range(2):
+        g_sib(piece, 1 - c).wait_recv()
     place(z)
 
     def g_take(step):
         src = lax.rem(z + n_track - 1 - step, n_track)
-        for part in range(2):
-            g_copy(step, src, src, part, part, part).wait_recv()
+        for piece in range(2):
+            for part in range(2):
+                g_copy(step, piece, src, src, part, part, part).wait_recv()
         place(src)
 
     each(n_track - 1, g_take)
 
-    half_ch = tg_ref.shape[1]
+    half_ch = tg_hbm.shape[1]
     theirs = pl.multiple_of((1 - c) * half_ch, half_ch)
     mine = pl.multiple_of(c * half_ch, half_ch)
 
     def t_copy(f, t):
-        return pltpu.make_async_remote_copy(src_ref=tgs_ref.at[f, pl.ds(theirs, half_ch), :], dst_ref=tg_ref.at[t],
+        return pltpu.make_async_remote_copy(src_ref=tgs_ref.at[f, pl.ds(theirs, half_ch), :], dst_ref=tg_hbm.at[t],
                                             send_sem=t_ssem.at[f], recv_sem=t_rsem.at[f], device_id=sib,
                                             device_id_type=MESH)
+
+    def o_copy(f):
+        return pltpu.make_async_copy(tgs_ref.at[f, pl.ds(mine, half_ch), :], tg_hbm.at[c * 4 + f], out_sem.at[f])
 
     for f in range(4):
         tgs_ref[f] = mm(qt_ref[...], gm_ref[f]) * scale
         t_copy(f, c * 4 + f).start()
-        tg_ref[c * 4 + f] = tgs_ref[f, pl.ds(mine, half_ch), :]
+        o_copy(f).start()
 
     each(n_track - 1, lambda step: q_copy(step, z).wait_send())
     h_copy.wait_send()
     x_copy.wait_send()
-    sib_copy(sendw_ref.at[z, 1 - c], recvw_ref.at[me], w_ssem, w_rsem).wait_send()
-    sib_copy(gs_ref.at[1 - c], recvg_ref.at[me], g_ssem, g_rsem).wait_send()
+    for piece in range(2):
+        w_sib(piece, c).wait_send()
+        g_sib(piece, c).wait_send()
 
     def sent(step):
         to = lax.rem(z + step + 1, n_track)
-        for part in range(2):
-            w_copy(step, to, z, part, c, c).wait_send()
-            g_copy(step, to, z, part, c, c).wait_send()
+        for piece in range(2):
+            for part in range(2):
+                w_copy(step, piece, to, z, part, c, c).wait_send()
+                g_copy(step, piece, to, z, part, c, c).wait_send()
 
     each(n_track - 1, sent)
+    upd_copy.wait()
     for f in range(4):
         t_copy(f, c * 4 + f).wait_send()
         t_copy(f, (1 - c) * 4 + f).wait_recv()
-
-
-def hand_out(upd_ref, tg_ref, upd_out, tg_out, sem):
-    copies = [pltpu.make_async_copy(tg_ref, tg_out, sem.at[0]), pltpu.make_async_copy(upd_ref, upd_out, sem.at[1])]
-    for copy in copies:
-        copy.start()
-    for copy in copies:
-        copy.wait()
+        o_copy(f).wait()
 
 
 def on_device(tokens, track_query, feature_map, tile_ids, corners, mlp_in, mlp_out, cotangent):
@@ -357,27 +376,28 @@
         functools.partial(kernel, n_track),
         out_shape=outs,
         in_specs=[pl.BlockSpec(memory_space=pltpu.HBM)] * 8,
-        out_specs=(pl.BlockSpec(memory_space=vmem), pl.BlockSpec(memory_space=vmem)),
+        out_specs=(pl.BlockSpec(memory_space=pltpu.HBM), pl.BlockSpec(memory_space=pltpu.HBM)),
         scratch_shapes=[vmem(arg.shape, arg.dtype) for arg in args] + [
             vmem((n_track, 80, 128), BF),
             vmem((4, all_tracks, pixels), F32),
             vmem((4, all_tracks, 128), I32),
             vmem((4, 2, all_tracks, 128), I32),
-            vmem((n_track, 2, 64, 128), BF),
-            vmem((peers, 64, 128), BF),
-            vmem((2, 128, 128), BF),
+            vmem((n_track, 2, 2, 32, 128), BF),
+            vmem((peers, 2, 32, 128), BF),
+            vmem((2, 2, 64, 128), BF),
             vmem((256, hid), BF),
             vmem((256, hid), BF),
             vmem((256, hid), BF),
-            vmem((2, 64, 128), BF),
-            vmem((peers, 64, 128), BF),
+            vmem((2, 2, 32, 128), BF),
+            vmem((peers, 2, 32, 128), BF),
             vmem((4, all_tracks, pixels), BF),
             vmem((channels, all_tracks), BF),
             vmem((4, channels, pixels), F32),
-            dma((8,)),
+            vmem((rows, width), BF),
+            dma((8,)), dma((5,)),
             dma((n_track - 1,)), dma((n_track - 1,)),
-            dma((peers,)), dma((peers,)),
-            dma((peers,)), dma((peers,)),
+            dma((2, peers)), dma((2, peers)),
+            dma((2, peers)), dma((2, peers)),
             dma, dma, dma, dma,
             dma((4,)), dma((4,)),
         ],
@@ -386,14 +406,6 @@
         cost_estimate=pl.CostEstimate(flops=10**9, bytes_accessed=4 * 10**6, transcendentals=2 * 10**5),
         name="corr_step",
     )(*[pltpu.with_memory_space_constraint(arg, pltpu.HBM) for arg in args])
-    upd, tg = pl.pallas_call(
-        hand_out,
-        out_shape=outs,
-        in_specs=[pl.BlockSpec(memory_space=vmem)] * 2,
-        out_specs=(pl.BlockSpec(memory_space=pltpu.HBM), pl.BlockSpec(memory_space=pltpu.HBM)),
-        scratch_shapes=[dma((2,))],
-        name="hand_out",
-    )(upd, tg)
     return upd.reshape(tokens.shape), jnp.transpose(tg, (0, 2, 1))
 
 

time: 25.7 us -> 24.1 us (0.938)
  Pallas kernels: 23.4 us -> 21.8 us
    pallas_call x1 -> x0, Pallas kernels: 2.01 us -> none  [on_device(): pl.pallas_call(hand_out, out_shape=outs, in_specs=[pl.BlockSpec(memory_sp...]
    pallas_call x1, Pallas kernels: 21.4 us -> 21.8 us  [on_device(): pl.pallas_call(functools.partial(kernel, n_track), out_shape=outs, in_spe...]
    unnamed x4 -> x2, local copies, waits for them, and re-layouts: 1.47 us -> 1.5 us
where the time goes in v3:
time: 24.1 us; the launch traced here: 23.9 us
  Pallas kernels  21.8 us (90%)
  local copies, waits for them, and re-layouts  1.5 us (6%)
  between operations  0.64 us (3%)
    pallas_call x1, Pallas kernels, on_device(): pl.pallas_call(functools.partial(kernel, n_track), out_shape=outs, in_spe...  21.8 us
    unnamed x2, local copies, waits for them, and re-layouts  1.5 us

profile of v3, /device:TPU:0, one launch (start us, length us, event | category | flops | bytes accessed | tf_op | source)
XLA Modules:
  0.0 23.9 jit_solution(12826840163453132233)
XLA Ops:
  0.6 21.8 %corr_step.1 = (bf16[512,192]{1,0:T(8,128)(2,1)S(1)}, f32[8,64,256]{2,1,0:T(8,128)S(1)}) custom-call(bf16[512,192]{1,0:T(8,128)(2,1)} %bitcast.15, bf16[64,128]{1,0:T(8,128)(2,1)} %qry_hbm.1, bf16[8,256,128]{2,1,0:T(8,128)(2,1)} %fmap_hbm.1, s32[8,1,64]{2,1,0:T(1,128)} %bitcast.18, s32[8,64]{1,0:T(8,128)} %bitcast.19, bf16[49,384]{1,0:T(8,128)(2,1)} %win_hbm.1, ...), custom_call_target="tpu_custom_call" | custom-call | flops 1000000000 | bytes 4000000 | tf_op jit(solution)/shard_map/corr_step/pallas_call | solution.py:375
  22.4 0.7 %copy.13 = bf16[64,8,192]{2,1,0:T(8,128)(2,1)} copy(bf16[64,8,192]{2,1,0:T(8,128)(2,1)S(1)} %bitcast.14) | data formatting | bytes 393216
  23.1 0.8 %copy.14 = f32[8,256,64]{1,2,0:T(8,128)} copy(f32[8,256,64]{1,2,0:T(8,128)S(1)} %bitcast.13) | data formatting | bytes 1048576

commit v4 on v2

--- a/solution.py
+++ b/solution.py
@@ -55,11 +55,11 @@
 
 
 def kernel(n_track, tok_hbm, qry_hbm, fmap_hbm, tile_hbm, corner_hbm, win_hbm, wout_hbm, cot_hbm,
-           upd_ref, tg_ref,
+           upd_hbm, tg_hbm,
            tok_ref, qry_ref, fmap_ref, tile_ref, corner_ref, win_ref, wout_ref, cot_ref,
            qb_ref, corr_ref, loc_ref, wi_ref, sendw_ref, recvw_ref, xs_ref, gh_ref, ghs_ref, gho_ref, gs_ref,
-           recvg_ref, gm_ref, qt_ref, tgs_ref,
-           in_sem, q_ssem, q_rsem, w_ssem, w_rsem, g_ssem, g_rsem, x_ssem, x_rsem, h_ssem, h_rsem, t_ssem, t_rsem):
+           recvg_ref, gm_ref, qt_ref, tgs_ref, upd_ref,
+           in_sem, out_sem, q_ssem, q_rsem, w_ssem, w_rsem, g_ssem, g_rsem, x_ssem, x_rsem, h_ssem, h_rsem, t_ssem, t_rsem):
     loads = [pltpu.make_async_copy(src, dst, in_sem.at[i]) for i, (src, dst) in enumerate((
         (tile_hbm, tile_ref), (corner_hbm, corner_ref), (qry_hbm, qry_ref), (cot_hbm, cot_ref), (wout_hbm, wout_ref),
         (fmap_hbm, fmap_ref), (win_hbm, win_ref), (tok_hbm, tok_ref)))]
@@ -103,7 +103,7 @@
 
     each(n_track - 1, lambda step: q_copy(step, z).start())
 
-    for load in loads[3:]:
+    for load in loads[3:5]:
         load.wait()
     wout = wout_ref[...]
     rows = 256
@@ -114,6 +114,9 @@
                                           device_id=sib, device_id_type=MESH)
     h_copy.start()
     gho_ref[...] = mm(cot_ref[pl.ds(own, rows), :], wout).astype(BF)
+
+    for load in loads[5:]:
+        load.wait()
 
     wst = mm(onehot((iota((128, 49), 0) & 63) == iota((128, 49), 1)), win_ref[...]).astype(BF)
 
@@ -271,6 +274,8 @@
     pre = first_layer(1)
     sq, th = gelu_parts(pre)
     finish(pre, th, oth)
+    upd_copy = pltpu.make_async_copy(upd_ref, upd_hbm, out_sem.at[4])
+    upd_copy.start()
 
     def place(src):
         r0 = pl.multiple_of(src * 64, 64)
@@ -293,19 +298,22 @@
 
     each(n_track - 1, g_take)
 
-    half_ch = tg_ref.shape[1]
+    half_ch = tg_hbm.shape[1]
     theirs = pl.multiple_of((1 - c) * half_ch, half_ch)
     mine = pl.multiple_of(c * half_ch, half_ch)
 
     def t_copy(f, t):
-        return pltpu.make_async_remote_copy(src_ref=tgs_ref.at[f, pl.ds(theirs, half_ch), :], dst_ref=tg_ref.at[t],
+        return pltpu.make_async_remote_copy(src_ref=tgs_ref.at[f, pl.ds(theirs, half_ch), :], dst_ref=tg_hbm.at[t],
                                             send_sem=t_ssem.at[f], recv_sem=t_rsem.at[f], device_id=sib,
                                             device_id_type=MESH)
+
+    def o_copy(f):
+        return pltpu.make_async_copy(tgs_ref.at[f, pl.ds(mine, half_ch), :], tg_hbm.at[c * 4 + f], out_sem.at[f])
 
     for f in range(4):
         tgs_ref[f] = mm(qt_ref[...], gm_ref[f]) * scale
         t_copy(f, c * 4 + f).start()
-        tg_ref[c * 4 + f] = tgs_ref[f, pl.ds(mine, half_ch), :]
+        o_copy(f).start()
 
     each(n_track - 1, lambda step: q_copy(step, z).wait_send())
     h_copy.wait_send()
@@ -320,17 +328,11 @@
             g_copy(step, to, z, part, c, c).wait_send()
 
     each(n_track - 1, sent)
+    upd_copy.wait()
     for f in range(4):
         t_copy(f, c * 4 + f).wait_send()
         t_copy(f, (1 - c) * 4 + f).wait_recv()
-
-
-def hand_out(upd_ref, tg_ref, upd_out, tg_out, sem):
-    copies = [pltpu.make_async_copy(tg_ref, tg_out, sem.at[0]), pltpu.make_async_copy(upd_ref, upd_out, sem.at[1])]
-    for copy in copies:
-        copy.start()
-    for copy in copies:
-        copy.wait()
+        o_copy(f).wait()
 
 
 def on_device(tokens, track_query, feature_map, tile_ids, corners, mlp_in, mlp_out, cotangent):
@@ -357,7 +359,7 @@
         functools.partial(kernel, n_track),
         out_shape=outs,
         in_specs=[pl.BlockSpec(memory_space=pltpu.HBM)] * 8,
-        out_specs=(pl.BlockSpec(memory_space=vmem), pl.BlockSpec(memory_space=vmem)),
+        out_specs=(pl.BlockSpec(memory_space=pltpu.HBM), pl.BlockSpec(memory_space=pltpu.HBM)),
         scratch_shapes=[vmem(arg.shape, arg.dtype) for arg in args] + [
             vmem((n_track, 80, 128), BF),
             vmem((4, all_tracks, pixels), F32),
@@ -374,7 +376,8 @@
             vmem((4, all_tracks, pixels), BF),
             vmem((channels, all_tracks), BF),
             vmem((4, channels, pixels), F32),
-            dma((8,)),
+            vmem((rows, width), BF),
+            dma((8,)), dma((5,)),
             dma((n_track - 1,)), dma((n_track - 1,)),
             dma((peers,)), dma((peers,)),
             dma((peers,)), dma((peers,)),
@@ -386,14 +389,6 @@
         cost_estimate=pl.CostEstimate(flops=10**9, bytes_accessed=4 * 10**6, transcendentals=2 * 10**5),
         name="corr_step",
     )(*[pltpu.with_memory_space_constraint(arg, pltpu.HBM) for arg in args])
-    upd, tg = pl.pallas_call(
-        hand_out,
-        out_shape=outs,
-        in_specs=[pl.BlockSpec(memory_space=vmem)] * 2,
-        out_specs=(pl.BlockSpec(memory_space=pltpu.HBM), pl.BlockSpec(memory_space=pltpu.HBM)),
-        scratch_shapes=[dma((2,))],
-        name="hand_out",
-    )(upd, tg)
     return upd.reshape(tokens.shape), jnp.transpose(tg, (0, 2, 1))
 
 

time: 25.7 us -> 24 us (0.934)
  Pallas kernels: 23.4 us -> 21.7 us
    pallas_call x1 -> x0, Pallas kernels: 2.01 us -> none  [on_device(): pl.pallas_call(hand_out, out_shape=outs, in_specs=[pl.BlockSpec(memory_sp...]
    pallas_call x1, Pallas kernels: 21.4 us -> 21.7 us  [on_device(): pl.pallas_call(functools.partial(kernel, n_track), out_shape=outs, in_spe...]
    unnamed x4 -> x2, local copies, waits for them, and re-layouts: 1.47 us -> 1.5 us
where the time goes in v4:
time: 24 us; the launch traced here: 23.8 us
  Pallas kernels  21.7 us (90%)
  local copies, waits for them, and re-layouts  1.5 us (6%)
  between operations  0.64 us (3%)
    pallas_call x1, Pallas kernels, on_device(): pl.pallas_call(functools.partial(kernel, n_track), out_shape=outs, in_spe...  21.7 us
    unnamed x2, local copies, waits for them, and re-layouts  1.5 us

profile of v4, /device:TPU:0, one launch (start us, length us, event | category | flops | bytes accessed | tf_op | source)
XLA Modules:
  0.0 23.8 jit_solution(13149486674020053158)
XLA Ops:
  0.6 21.7 %corr_step.1 = (bf16[512,192]{1,0:T(8,128)(2,1)S(1)}, f32[8,64,256]{2,1,0:T(8,128)S(1)}) custom-call(bf16[512,192]{1,0:T(8,128)(2,1)} %bitcast.15, bf16[64,128]{1,0:T(8,128)(2,1)} %qry_hbm.1, bf16[8,256,128]{2,1,0:T(8,128)(2,1)} %fmap_hbm.1, s32[8,1,64]{2,1,0:T(1,128)} %bitcast.18, s32[8,64]{1,0:T(8,128)} %bitcast.19, bf16[49,384]{1,0:T(8,128)(2,1)} %win_hbm.1, ...), custom_call_target="tpu_custom_call" | custom-call | flops 1000000000 | bytes 4000000 | tf_op jit(solution)/shard_map/corr_step/pallas_call | solution.py:358
  22.3 0.7 %copy.13 = bf16[64,8,192]{2,1,0:T(8,128)(2,1)} copy(bf16[64,8,192]{2,1,0:T(8,128)(2,1)S(1)} %bitcast.14) | data formatting | bytes 393216
  23.0 0.8 %copy.14 = f32[8,256,64]{1,2,0:T(8,128)} copy(f32[8,256,64]{1,2,0:T(8,128)S(1)} %bitcast.13) | data formatting | bytes 1048576

commit v5 on v4

--- a/solution.py
+++ b/solution.py
@@ -75,6 +75,15 @@
     chunk_rows = group * 64
     n_chunks = n_track // group
 
+    def gap(step):
+        return 1 + lax.rem(jnp.int32(step + n_track // 2 - 1), jnp.int32(n_track - 1))
+
+    def ahead(step):
+        return lax.rem(z + gap(step), n_track)
+
+    def behind(step):
+        return lax.rem(z + n_track - gap(step), n_track)
+
     barrier = pltpu.get_barrier_semaphore()
 
     def greet(step):
@@ -99,7 +108,7 @@
     def q_copy(step, slot):
         return pltpu.make_async_remote_copy(
             src_ref=qb_ref.at[slot], dst_ref=qb_ref.at[slot], send_sem=q_ssem.at[step], recv_sem=q_rsem.at[step],
-            device_id={"track": lax.rem(z + step + 1, n_track)}, device_id_type=MESH)
+            device_id={"track": ahead(step)}, device_id_type=MESH)
 
     each(n_track - 1, lambda step: q_copy(step, z).start())
 
@@ -120,7 +129,7 @@
 
     wst = mm(onehot((iota((128, 49), 0) & 63) == iota((128, 49), 1)), win_ref[...]).astype(BF)
 
-    each(n_track - 1, lambda step: q_copy(step, lax.rem(z + n_track - 1 - step, n_track)).wait_recv())
+    each(n_track - 1, lambda step: q_copy(step, behind(step)).wait_recv())
 
     lane = iota((64, 128), 1)
     low = lane < 64
@@ -167,7 +176,7 @@
             sendw_ref[to, :, j * 32:(j + 1) * 32, :] = val.reshape(2, 32, 128)
 
     def w_send(step):
-        to = lax.rem(z + step + 1, n_track)
+        to = ahead(step)
         windows(to)
         for part in range(2):
             w_copy(step, to, z, part, c, c).start()
@@ -216,7 +225,7 @@
     fold = onehot(q_row == ((u_of >> 2) << 6) + ((u_of & 1) << 5) + (q_col >> 3))
 
     def w_wait(step):
-        src = lax.rem(z + n_track - 1 - step, n_track)
+        src = behind(step)
         for part in range(2):
             w_copy(step, src, src, part, part, part).wait_recv()
 
@@ -263,7 +272,7 @@
 
     def g_send(step):
         for part in range(2):
-            g_copy(step, lax.rem(z + step + 1, n_track), z, part, c, c).start()
+            g_copy(step, ahead(step), z, part, c, c).start()
 
     each(n_track - 1, g_send)
     sib_copy(gs_ref.at[1 - c], recvg_ref.at[me], g_ssem, g_rsem).start()
@@ -291,12 +300,12 @@
     place(z)
 
     def g_take(step):
-        src = lax.rem(z + n_track - 1 - step, n_track)
+        src = behind(step)
         for part in range(2):
             g_copy(step, src, src, part, part, part).wait_recv()
         place(src)
 
-    each(n_track - 1, g_take)
+    each(n_track - 1, lambda step: g_take(n_track - 2 - step))
 
     half_ch = tg_hbm.shape[1]
     theirs = pl.multiple_of((1 - c) * half_ch, half_ch)
@@ -322,7 +331,7 @@
     sib_copy(gs_ref.at[1 - c], recvg_ref.at[me], g_ssem, g_rsem).wait_send()
 
     def sent(step):
-        to = lax.rem(z + step + 1, n_track)
+        to = ahead(step)
         for part in range(2):
             w_copy(step, to, z, part, c, c).wait_send()
             g_copy(step, to, z, part, c, c).wait_send()

time: 24 us -> 24 us (level)
  no operation moved by 1% of the time
where the time goes in v5:
time: 24 us; the launch traced here: 23.8 us
  Pallas kernels  21.6 us (90%)
  local copies, waits for them, and re-layouts  1.5 us (6%)
  between operations  0.64 us (3%)
    pallas_call x1, Pallas kernels, on_device(): pl.pallas_call(functools.partial(kernel, n_track), out_shape=outs, in_spe...  21.6 us
    unnamed x2, local copies, waits for them, and re-layouts  1.5 us

profile of v5, /device:TPU:0, one launch (start us, length us, event | category | flops | bytes accessed | tf_op | source)
XLA Modules:
  0.0 23.8 jit_solution(3154104563030645166)
XLA Ops:
  0.6 21.6 %corr_step.1 = (bf16[512,192]{1,0:T(8,128)(2,1)S(1)}, f32[8,64,256]{2,1,0:T(8,128)S(1)}) custom-call(bf16[512,192]{1,0:T(8,128)(2,1)} %bitcast.15, bf16[64,128]{1,0:T(8,128)(2,1)} %qry_hbm.1, bf16[8,256,128]{2,1,0:T(8,128)(2,1)} %fmap_hbm.1, s32[8,1,64]{2,1,0:T(1,128)} %bitcast.18, s32[8,64]{1,0:T(8,128)} %bitcast.19, bf16[49,384]{1,0:T(8,128)(2,1)} %win_hbm.1, ...), custom_call_target="tpu_custom_call" | custom-call | flops 1000000000 | bytes 4000000 | tf_op jit(solution)/shard_map/corr_step/pallas_call | solution.py:367
  22.3 0.7 %copy.13 = bf16[64,8,192]{2,1,0:T(8,128)(2,1)} copy(bf16[64,8,192]{2,1,0:T(8,128)(2,1)S(1)} %bitcast.14) | data formatting | bytes 393216
  23.0 0.8 %copy.14 = f32[8,256,64]{1,2,0:T(8,128)} copy(f32[8,256,64]{1,2,0:T(8,128)S(1)} %bitcast.13) | data formatting | bytes 1048576
